TPU v7x, 128 devices: a whole 4x4x4 slice. The times are simulated.
128 devices in a mesh: row: 8 (over z_hi, y), col: 16 (over z_lo, x, core).
Axes of the slice: x: 4, y: 4, z: 4 (z_hi: 2, z_lo: 2; z = z_hi * 2 + z_lo), core: 2. Of those that a mesh axis runs over, the one named last changes fastest.
Arguments:
- band_vectors: float32 [65536, 4096], P(('row', 'col')), may hold values from -6 to 6
- reflectors: float32 [4, 65536, 256], P(None, 'row', 'col'), as said below
- t_factors: float32 [4, 256, 256], replicated, as said below
Outputs:
- back_vectors: float32 [65536, 4096], P('row', 'col')
Inputs may be any that keep to these rules, and one draw needn't show every extreme that they name: Each column of reflectors[k] has entries of order 65536^-0.5 and no zero column. t_factors[k] is upper triangular with diagonal entries between 1.6 and 2.4.
All inputs are finite; a program needn't handle non-finite values.
Results may differ from a plain program's by a relative error of at most 0.0001.
Values sent between devices are 32-bit elements; how exact they have to be, the bound alone decides.
No kernel may reach another device: no remote copies, remote signals or barrier semaphores. Data moves between devices by JAX's collectives and lax.ppermute only.
A program may use at most 192 MiB of HBM per device.

v0:
```python
import functools

import jax
import jax.numpy as jnp
from jax import lax
from jax.sharding import PartitionSpec as P

precise = lax.Precision.HIGHEST


def contract_rows(panels, vectors):
    return lax.dot_general(
        panels,
        vectors,
        (((1,), (0,)), ((), ())),
        precision=precise,
        preferred_element_type=jnp.float32,
    )


def expand_rows(panels, coeffs):
    return lax.dot_general(
        panels,
        coeffs,
        (((0, 2), (0, 1)), ((), ())),
        precision=precise,
        preferred_element_type=jnp.float32,
    )


def triangle_apply(factor, coeffs):
    stacked = coeffs.reshape(factor.shape[0], coeffs.shape[2])
    result = jnp.dot(factor, stacked, precision=precise, preferred_element_type=jnp.float32)
    return result.reshape(coeffs.shape)


def reduce_apply(partial_sums, apply_fn):
    return apply_fn(lax.psum(partial_sums, "row"))


def apply_panels(vectors, panels, t_factors):
    count = panels.shape[0]
    for index in reversed(range(count)):
        single = panels[index : index + 1]
        partial_sums = contract_rows(single, vectors)
        coeffs = reduce_apply(partial_sums, functools.partial(triangle_apply, t_factors[index]))
        vectors = vectors - expand_rows(single, coeffs)
    return vectors


def local(band_vectors, reflectors, t_factors):
    block = lax.all_to_all(band_vectors, "col", split_axis=1, concat_axis=0, tiled=True)
    panels = lax.all_gather(reflectors, "col", axis=2, tiled=True)
    return apply_panels(block, panels, t_factors)


def solution(mesh):
    in_specs = (P(("row", "col"), None), P(None, "row", "col"), P())
    out_specs = P("row", "col")
    return jax.shard_map(local, mesh=mesh, in_specs=in_specs, out_specs=out_specs, check_vma=False)
```

profile of v0, /device:TPU:1, one launch (start us, length us, event | category | flops | bytes accessed | tf_op | source)
XLA Modules:
  0.0 726.0 jit_solution(13109120159513075017)
XLA Ops:
  6.5 0.0 all-gather.2.cloned.1.call-start
  6.5 0.7 all-gather.2.cloned.1.call-update
  7.3 0.0 all-reduce.5.cloned.1.call-start
  7.3 8.9 %copy.6 = f32[512,4096]{0,1:T(8,128)} copy(f32[512,4096]{1,0:T(8,128)} %param.3) | data formatting | bytes 16777216 | tf_op args[0]
  16.3 188.6 %all_to_all.19 = f32[512,16,256]{0,2,1:T(8,128)S(1)} all-to-all(f32[512,16,256]{0,2,1:T(8,128)} %bitcast.75), channel_id=1, replica_groups=mesh['row'=8,'col'=16] {'col'}, dimensions={1} | all-to-all | bytes 16777216 | tf_op jit(solution)/shard_map/all_to_all | solution.py:52
  204.9 4.4 copy.9
  209.3 63.9 %all-gather.2.cloned.1.call-done = f32[4,8192,256]{1,2,0:T(8,128)} async-done(((f32[4,8192,16]{1,2,0:T(8,128)}), f32[4,8192,256]{1,2,0:T(8,128)}) %all-gather.2.cloned.1.call-update) | async-done | bytes 33554448 | tf_op jit(solution)/shard_map/all_gather | solution.py:53
  273.2 0.0 copy-start.3
  273.2 11.3 %fusion.4 = f32[256,256]{1,0:T(8,128)} fusion(f32[8192,256]{0,1:T(8,128)} %bitcast.72, f32[4,8192,256]{1,2,0:T(8,128)} %all-gather.2.cloned.1.call-done), kind=kOutput, calls=%fused_computation.12 | convolution fusion | flops 6442450944 | bytes 17039360 | tf_op jit(solution)/shard_map/dot_general | solution.py:12
  284.5 0.0 all-reduce.5.cloned.1.call-update
  284.6 0.2 all-reduce.7.cloned.1.call-start
  284.8 79.3 %all-reduce.5.cloned.1.call-done = f32[256,256]{1,0:T(8,128)} async-done(((f32[256,256]{1,0:T(8,128)}), f32[256,256]{1,0:T(8,128)}) %all-reduce.5.cloned.1.call-update) | async-done | bytes 262160 | tf_op jit(solution)/shard_map/psum | solution.py:38
  364.1 0.0 copy-done.3
  364.1 1.5 fusion.17
  365.7 11.9 %fusion.3 = f32[8192,256]{0,1:T(8,128)S(1)} fusion(f32[8192,256]{0,1:T(8,128)} %bitcast.73, f32[256,256]{1,0:T(8,128)S(1)} %fusion.17, f32[4,8192,256]{1,2,0:T(8,128)} %all-gather.2.cloned.1.call-done), kind=kOutput, calls=%fused_computation.7 | convolution fusion | flops 6444548096 | bytes 25427968 | tf_op jit(solution)/shard_map/dot_general | solution.py:22
  377.6 0.0 copy-start
  377.6 3.4 copy-done
  381.0 10.1 %fusion.10 = f32[256,256]{0,1:T(8,128)} fusion(f32[8192,256]{0,1:T(8,128)S(1)} %fusion.3, f32[4,8192,256]{1,2,0:T(8,128)} %all-gather.2.cloned.1.call-done), kind=kOutput, calls=%fused_computation.18 | convolution fusion | flops 6442450944 | bytes 17039360 | tf_op jit(solution)/shard_map/dot_general | solution.py:12
  391.1 0.0 all-reduce.7.cloned.1.call-update
  391.1 0.3 all-reduce.9.cloned.1.call-start
  391.4 82.4 %all-reduce.7.cloned.1.call-done = f32[256,256]{0,1:T(8,128)} async-done(((f32[256,256]{0,1:T(8,128)}), f32[256,256]{0,1:T(8,128)}) %all-reduce.7.cloned.1.call-update) | async-done | bytes 262160 | tf_op jit(solution)/shard_map/psum | solution.py:38
  473.7 1.4 fusion.15
  475.1 11.9 %fusion.2 = f32[8192,256]{0,1:T(8,128)S(1)} fusion(f32[8192,256]{0,1:T(8,128)} %copy-done, f32[256,256]{1,0:T(8,128)S(1)} %fusion.15, f32[4,8192,256]{1,2,0:T(8,128)} %all-gather.2.cloned.1.call-done), kind=kOutput, calls=%fused_computation.5 | convolution fusion | flops 6444548096 | bytes 25427968 | tf_op jit(solution)/shard_map/dot_general | solution.py:22
  487.0 0.0 copy-start.1
  487.0 3.4 copy-done.1
  490.4 10.1 %fusion.9 = f32[256,256]{0,1:T(8,128)} fusion(f32[8192,256]{0,1:T(8,128)S(1)} %fusion.2, f32[4,8192,256]{1,2,0:T(8,128)} %all-gather.2.cloned.1.call-done), kind=kOutput, calls=%fused_computation.17 | convolution fusion | flops 6442450944 | bytes 17039360 | tf_op jit(solution)/shard_map/dot_general | solution.py:12
  500.5 0.0 all-reduce.9.cloned.1.call-update
  500.5 0.3 all-reduce.11.cloned.1.call-start
  500.8 82.3 %all-reduce.9.cloned.1.call-done = f32[256,256]{0,1:T(8,128)} async-done(((f32[256,256]{0,1:T(8,128)}), f32[256,256]{0,1:T(8,128)}) %all-reduce.9.cloned.1.call-update) | async-done | bytes 262160 | tf_op jit(solution)/shard_map/psum | solution.py:38
  583.1 1.4 fusion.13
  584.5 11.9 %fusion.1 = f32[8192,256]{0,1:T(8,128)S(1)} fusion(f32[8192,256]{0,1:T(8,128)} %copy-done.1, f32[256,256]{1,0:T(8,128)S(1)} %fusion.13, f32[4,8192,256]{1,2,0:T(8,128)} %all-gather.2.cloned.1.call-done), kind=kOutput, calls=%fused_computation.3 | convolution fusion | flops 6444548096 | bytes 25427968 | tf_op jit(solution)/shard_map/dot_general | solution.py:22
  596.4 0.0 copy-start.2
  596.4 3.4 copy-done.2
  599.8 10.1 %fusion.8 = f32[256,256]{0,1:T(8,128)} fusion(f32[8192,256]{0,1:T(8,128)S(1)} %fusion.1, f32[4,8192,256]{1,2,0:T(8,128)} %all-gather.2.cloned.1.call-done), kind=kOutput, calls=%fused_computation.16 | convolution fusion | flops 6442450944 | bytes 17039360 | tf_op jit(solution)/shard_map/dot_general | solution.py:12
  609.9 0.0 all-reduce.11.cloned.1.call-update
  609.9 82.6 %all-reduce.11.cloned.1.call-done = f32[256,256]{0,1:T(8,128)} async-done(((f32[256,256]{0,1:T(8,128)}), f32[256,256]{0,1:T(8,128)}) %all-reduce.11.cloned.1.call-update) | async-done | bytes 262160 | tf_op jit(solution)/shard_map/psum | solution.py:38
  692.6 1.4 fusion.11
  693.9 16.5 %fusion = f32[8192,256]{0,1:T(8,128)} fusion(f32[8192,256]{0,1:T(8,128)} %copy-done.2, f32[256,256]{1,0:T(8,128)S(1)} %fusion.11, f32[4,8192,256]{1,2,0:T(8,128)} %all-gather.2.cloned.1.call-done), kind=kOutput, calls=%fused_computation.1 | convolution fusion | flops 6444548096 | bytes 25427968 | tf_op jit(solution)/shard_map/dot_general | solution.py:22
  710.5 9.0 %copy.8 = f32[8192,256]{1,0:T(8,128)} copy(f32[8192,256]{0,1:T(8,128)} %fusion) | data formatting | bytes 16777216 | tf_op jit(solution)/shard_map/sub | solution.py:47
Async XLA Ops:
  6.5 266.7 %all-gather.2.cloned.1.call-start = ((), (), s32[]{:S(2)}) async-start(), calls=%async_computation.1 | async-start | bytes 35651584 | tf_op jit(solution)/shard_map/all_gather | solution.py:53
  7.3 356.9 %all-reduce.5.cloned.1.call-start = ((), (), s32[]{:S(2)}) async-start(), calls=%async_computation.2 | async-start | bytes 524288 | tf_op jit(solution)/shard_map/psum | solution.py:38
  273.2 90.9 %copy-start.3 = (f32[4,256,256]{2,1,0:T(8,128)S(1)}, f32[4,256,256]{2,1,0:T(8,128)}, u32[]{:S(2)}) copy-start(f32[4,256,256]{2,1,0:T(8,128)} %param.5) | copy-start | bytes 3145732
  284.6 189.2 %all-reduce.7.cloned.1.call-start = ((), (), s32[]{:S(2)}) async-start(), calls=%async_computation.3 | async-start | bytes 524288 | tf_op jit(solution)/shard_map/psum | solution.py:38
  377.6 3.4 copy-start
  391.1 192.1 %all-reduce.9.cloned.1.call-start = ((), (), s32[]{:S(2)}) async-start(), calls=%async_computation.4 | async-start | bytes 524288 | tf_op jit(solution)/shard_map/psum | solution.py:38
  487.0 3.4 copy-start.1
  500.5 192.0 %all-reduce.11.cloned.1.call-start = ((), (), s32[]{:S(2)}) async-start(), calls=%async_computation.5 | async-start | bytes 524288 | tf_op jit(solution)/shard_map/psum | solution.py:38
  596.4 3.4 copy-start.2
Sparse Core Ops, SparseCore 0:
  9.0 264.1 all-gather.1
  284.7 79.3 all-reduce.4
  391.2 82.4 all-reduce.6
  500.6 82.4 all-reduce.8
  610.1 82.4 all-reduce.10
where the time goes:
time: 731 us; the launch traced here: 726 us
  waiting for transfers between devices  391 us (53%)
  blocking collectives  189 us (26%)
  matrix products  99.5 us (14%)
  local copies, waits for them, and re-layouts  32.5 us (4%)
  between operations  13.2 us (2%)
    psum x4, waiting for transfers between devices, reduce_apply(): return apply_fn(lax.psum(partial_sums, 'row'))  327 us
    all_to_all x1, blocking collectives, local(): lax.all_to_all(band_vectors, 'col', split_axis=1, concat_axis=0, tiled=True)  189 us
    all_gather x1, waiting for transfers between devices, local(): panels = lax.all_gather(reflectors, 'col', axis=2, tiled=True)  63.9 us
    dot_general x4, matrix products, expand_rows(): lax.dot_general(panels, coeffs, (((0, 2), (0, 1)), ((), ())), precision=p...  52.2 us
    dot_general x4, matrix products, contract_rows(): lax.dot_general(panels, vectors, (((1,), (0,)), ((), ())), precision=prec...  41.6 us
    unnamed x9, local copies, waits for them, and re-layouts  19.1 us
  transfers between devices with their start and end apart: 5, of which 5 were waited for; matrix products, arithmetic and copies ran while one was open for 2% of the time, Pallas kernels for 0%

commit v1 on v0

v1 whole, which is shorter than its diff:
```python
import jax
import jax.numpy as jnp
from jax import lax
from jax.sharding import PartitionSpec as P

HIGH = lax.Precision.HIGH
HIGHEST = lax.Precision.HIGHEST


def dot(a, b, dims, precision):
    return lax.dot_general(a, b, (dims, ((), ())), precision=precision, preferred_element_type=jnp.float32)


def sum_rows(values, size):
    slices = values.reshape(size, values.shape[0] // size, values.shape[1])
    mine = lax.all_to_all(slices, "row", split_axis=0, concat_axis=0, tiled=True).sum(0)
    copies = jnp.broadcast_to(mine[None], slices.shape)
    return lax.all_to_all(copies, "row", split_axis=0, concat_axis=0, tiled=True).reshape(values.shape)


def solution(mesh):
    row_size = mesh.shape["row"]

    def local(band_vectors, reflectors, t_factors):
        count = reflectors.shape[0]
        own = jnp.swapaxes(reflectors, 1, 2)
        panels = [None] * count
        for k in reversed(range(count)):
            panels[k] = lax.all_gather(own[k], "col", axis=0, tiled=True)
        vectors = lax.all_to_all(band_vectors, "col", split_axis=1, concat_axis=0, tiled=True)
        for k in reversed(range(count)):
            sums = sum_rows(dot(panels[k], vectors, ((1,), (0,)), HIGH), row_size)
            coeffs = dot(t_factors[k], sums, ((1,), (0,)), HIGHEST)
            vectors = vectors - dot(panels[k], coeffs, ((0,), (0,)), HIGH)
        return vectors

    in_specs = (P(("row", "col"), None), P(None, "row", "col"), P())
    return jax.shard_map(local, mesh=mesh, in_specs=in_specs, out_specs=P("row", "col"), check_vma=False)
```

time: 731 us -> 398 us (0.54)
  waiting for transfers between devices: 391 us -> 28 us
  blocking collectives: 189 us -> 242 us
  local copies, waits for them, and re-layouts: 32.5 us -> 7.13 us
    psum x4 -> x0, waiting for transfers between devices: 327 us -> none  [reduce_apply(): return apply_fn(lax.psum(partial_sums, 'row'))]
    all_to_all x0 -> x8, blocking collectives: none -> 103 us  [the longest x4 60.4 us: sum_rows(): lax.all_to_all(slices, 'row', split_axis=0, concat_axis=0, tiled=True)]
    all_to_all x1, blocking collectives: 189 us -> 138 us  [local(): lax.all_to_all(band_vectors, 'col', split_axis=1, concat_axis=0, tiled=True)]
    all_gather x1 -> x4, waiting for transfers between devices: 63.9 us -> 26.1 us  [local(): panels[k] = lax.all_gather(own[k], 'col', axis=0, tiled=True)]
    unnamed x9 -> x2, local copies, waits for them, and re-layouts: 19.1 us -> 0.01 us
    sub x1 -> x0, local copies, waits for them, and re-layouts: 8.99 us -> none  [apply_panels(): vectors = vectors - expand_rows(single, coeffs)]
  transfers between devices with their start and end apart: 5 -> 4, of which waited for: 5 -> 3; matrix products, arithmetic and copies ran while one was open for 2% -> 21% of each run, Pallas kernels for 0% -> 0%
where the time goes in v1:
time: 398 us; the launch traced here: 393 us
  blocking collectives  242 us (61%)
  matrix products  103 us (26%)
  waiting for transfers between devices  28 us (7%)
  between operations  13.5 us (3%)
  local copies, waits for them, and re-layouts  7.13 us (2%)
    all_to_all x1, blocking collectives, local(): lax.all_to_all(band_vectors, 'col', split_axis=1, concat_axis=0, tiled=True)  138 us
    dot_general x12, matrix products, dot(): lax.dot_general(a, b, (dims, ((), ())), precision=precision, preferred_el...  103 us
    all_to_all x4, blocking collectives, sum_rows(): lax.all_to_all(slices, 'row', split_axis=0, concat_axis=0, tiled=True)  60.4 us
    all_to_all x4, blocking collectives, sum_rows(): lax.all_to_all(copies, 'row', split_axis=0, concat_axis=0, tiled=True)  42.8 us
    all_gather x4, waiting for transfers between devices, local(): panels[k] = lax.all_gather(own[k], 'col', axis=0, tiled=True)  26.1 us
  transfers between devices with their start and end apart: 4, of which 3 were waited for; matrix products, arithmetic and copies ran while one was open for 21% of the time, Pallas kernels for 0%

profile of v1, /device:TPU:1, one launch (start us, length us, event | category | flops | bytes accessed | tf_op | source)
XLA Modules:
  0.0 393.4 jit_solution(9209260760785935637)
XLA Ops:
  6.5 0.0 all-gather.9.cloned.1.call-start
  6.5 2.9 fusion.26
  9.4 0.0 all-gather.9.cloned.1.call-update
  9.4 0.0 all-gather.11.cloned.1.call-start
  9.5 0.7 all-gather.11.cloned.1.call-update
  10.2 0.0 all-gather.13.cloned.1.call-start
  10.2 0.7 all-gather.13.cloned.1.call-update
  10.9 0.0 all-gather.15.cloned.1.call-start
  11.0 0.5 all-gather.15.cloned.1.call-update
  11.5 4.2 %copy.15 = f32[64,16,8,256]{3,2,0,1:T(8,128)S(1)} copy(f32[64,16,8,256]{3,2,1,0:T(8,128)} %bitcast.87) | data formatting | bytes 16777216 | tf_op jit(solution)/shard_map/all_to_all | solution.py:30
  15.7 138.5 %all_to_all.59 = f32[512,16,256]{2,0,1:T(8,128)} all-to-all(f32[512,16,256]{2,0,1:T(8,128)S(1)} %bitcast.86), channel_id=1, replica_groups=mesh['row'=8,'col'=16] {'col'}, dimensions={1} | all-to-all | bytes 16777216 | tf_op jit(solution)/shard_map/all_to_all | solution.py:30
  154.1 0.0 all-gather.9.cloned.1.call-done
  154.1 0.0 copy-start
  154.1 9.4 %fusion.27 = f32[8,32,256]{2,1,0:T(8,128)S(1)} fusion(f32[8,32,8192]{2,1,0:T(8,128)} %bitcast.85, f32[8192,256,1]{1,0,2:T(8,128)} %bitcast.83), kind=kOutput, calls=%fused_computation.32 | convolution fusion | flops 3221225472 | bytes 17039360 | tf_op jit(solution)/shard_map/dot_general | solution.py:11
  163.6 15.3 %all_to_all.60 = f32[8,32,256]{2,1,0:T(8,128)S(1)} all-to-all(f32[8,32,256]{2,1,0:T(8,128)S(1)} %fusion.27), channel_id=1, replica_groups=mesh['row'=8,'col'=16] {'row'}, dimensions={0} | all-to-all | bytes 524288 | tf_op jit(solution)/shard_map/all_to_all | solution.py:16
  178.9 11.0 %all_to_all.61 = f32[8,32,256]{2,1,0:T(8,128)S(1)} all-to-all(f32[8,32,256]{2,1,0:T(8,128)S(1)} %broadcast_in_dim.8), channel_id=1, replica_groups=mesh['row'=8,'col'=16] {'row'}, dimensions={0} | all-to-all | bytes 524288 | tf_op jit(solution)/shard_map/all_to_all | solution.py:18
  189.9 0.0 copy-done
  189.9 0.6 fusion.20
  190.5 16.1 %fusion.3 = f32[8192,256]{1,0:T(8,128)} fusion(f32[8192,256]{1,0:T(8,128)} %bitcast.84, f32[256,256]{1,0:T(8,128)S(1)} %fusion.20, f32[1,256,8192]{2,1,0:T(8,128)} %all-gather.9.cloned.1.call-done), kind=kOutput, calls=%fused_computation.7 | convolution fusion | flops 3223322624 | bytes 25427968 | tf_op jit(solution)/shard_map/dot_general | solution.py:11
  206.7 8.9 %all-gather.11.cloned.1.call-done = f32[1,256,8192]{2,1,0:T(8,128)} async-done(((f32[1,16,8192]{2,1,0:T(8,128)}), f32[1,256,8192]{2,1,0:T(8,128)}) %all-gather.11.cloned.1.call-update) | async-done | bytes 8388624 | tf_op jit(solution)/shard_map/all_gather | solution.py:29
  215.6 8.9 %fusion.11 = f32[256,256]{0,1:T(8,128)S(1)} fusion(f32[8192,256]{1,0:T(8,128)} %fusion.3, f32[1,256,8192]{2,1,0:T(8,128)} %all-gather.11.cloned.1.call-done), kind=kOutput, calls=%fused_computation.16 | convolution fusion | flops 3221225472 | bytes 17039360 | tf_op jit(solution)/shard_map/dot_general | solution.py:11
  224.5 15.0 %all_to_all.62 = f32[8,32,256]{2,1,0:T(8,128)S(1)} all-to-all(f32[8,32,256]{2,1,0:T(8,128)S(1)} %bitcast.89), channel_id=1, replica_groups=mesh['row'=8,'col'=16] {'row'}, dimensions={0} | all-to-all | bytes 524288 | tf_op jit(solution)/shard_map/all_to_all | solution.py:16
  239.6 10.7 %all_to_all.63 = f32[8,32,256]{2,1,0:T(8,128)S(1)} all-to-all(f32[8,32,256]{2,1,0:T(8,128)S(1)} %broadcast_in_dim.9), channel_id=1, replica_groups=mesh['row'=8,'col'=16] {'row'}, dimensions={0} | all-to-all | bytes 524288 | tf_op jit(solution)/shard_map/all_to_all | solution.py:18
  250.2 0.6 fusion.18
  250.9 16.2 %fusion.2 = f32[8192,256]{1,0:T(8,128)} fusion(f32[8192,256]{1,0:T(8,128)} %fusion.3, f32[256,256]{1,0:T(8,128)S(1)} %fusion.18, f32[1,256,8192]{2,1,0:T(8,128)} %all-gather.11.cloned.1.call-done), kind=kOutput, calls=%fused_computation.5 | convolution fusion | flops 3223322624 | bytes 25427968 | tf_op jit(solution)/shard_map/dot_general | solution.py:11
  267.0 8.7 %all-gather.13.cloned.1.call-done = f32[1,256,8192]{2,1,0:T(8,128)} async-done(((f32[1,16,8192]{2,1,0:T(8,128)}), f32[1,256,8192]{2,1,0:T(8,128)}) %all-gather.13.cloned.1.call-update) | async-done | bytes 8388624 | tf_op jit(solution)/shard_map/all_gather | solution.py:29
  275.7 8.9 %fusion.8 = f32[256,256]{0,1:T(8,128)S(1)} fusion(f32[8192,256]{1,0:T(8,128)} %fusion.2, f32[1,256,8192]{2,1,0:T(8,128)} %all-gather.13.cloned.1.call-done), kind=kOutput, calls=%fused_computation.13 | convolution fusion | flops 3221225472 | bytes 17039360 | tf_op jit(solution)/shard_map/dot_general | solution.py:11
  284.6 15.0 %all_to_all.64 = f32[8,32,256]{2,1,0:T(8,128)S(1)} all-to-all(f32[8,32,256]{2,1,0:T(8,128)S(1)} %bitcast.90), channel_id=1, replica_groups=mesh['row'=8,'col'=16] {'row'}, dimensions={0} | all-to-all | bytes 524288 | tf_op jit(solution)/shard_map/all_to_all | solution.py:16
  299.7 10.7 %all_to_all.65 = f32[8,32,256]{2,1,0:T(8,128)S(1)} all-to-all(f32[8,32,256]{2,1,0:T(8,128)S(1)} %broadcast_in_dim.10), channel_id=1, replica_groups=mesh['row'=8,'col'=16] {'row'}, dimensions={0} | all-to-all | bytes 524288 | tf_op jit(solution)/shard_map/all_to_all | solution.py:18
  310.4 0.6 fusion.16
  311.0 16.2 %fusion.1 = f32[8192,256]{1,0:T(8,128)} fusion(f32[8192,256]{1,0:T(8,128)} %fusion.2, f32[256,256]{1,0:T(8,128)S(1)} %fusion.16, f32[1,256,8192]{2,1,0:T(8,128)} %all-gather.13.cloned.1.call-done), kind=kOutput, calls=%fused_computation.3 | convolution fusion | flops 3223322624 | bytes 25427968 | tf_op jit(solution)/shard_map/dot_general | solution.py:11
  327.2 8.5 %all-gather.15.cloned.1.call-done = f32[1,256,8192]{2,1,0:T(8,128)} async-done(((f32[1,16,8192]{2,1,0:T(8,128)}), f32[1,256,8192]{2,1,0:T(8,128)}) %all-gather.15.cloned.1.call-update) | async-done | bytes 8388624 | tf_op jit(solution)/shard_map/all_gather | solution.py:29
  335.7 8.9 %fusion.5 = f32[256,256]{0,1:T(8,128)S(1)} fusion(f32[8192,256]{1,0:T(8,128)} %fusion.1, f32[1,256,8192]{2,1,0:T(8,128)} %all-gather.15.cloned.1.call-done), kind=kOutput, calls=%fused_computation.10 | convolution fusion | flops 3221225472 | bytes 17039360 | tf_op jit(solution)/shard_map/dot_general | solution.py:11
  344.6 15.0 %all_to_all.66 = f32[8,32,256]{2,1,0:T(8,128)S(1)} all-to-all(f32[8,32,256]{2,1,0:T(8,128)S(1)} %bitcast.91), channel_id=1, replica_groups=mesh['row'=8,'col'=16] {'row'}, dimensions={0} | all-to-all | bytes 524288 | tf_op jit(solution)/shard_map/all_to_all | solution.py:16
  359.7 10.5 %all_to_all.67 = f32[8,32,256]{2,1,0:T(8,128)S(1)} all-to-all(f32[8,32,256]{2,1,0:T(8,128)S(1)} %broadcast_in_dim.11), channel_id=1, replica_groups=mesh['row'=8,'col'=16] {'row'}, dimensions={0} | all-to-all | bytes 524288 | tf_op jit(solution)/shard_map/all_to_all | solution.py:18
  370.2 0.6 fusion.14
  370.8 15.9 %fusion = f32[8192,256]{1,0:T(8,128)} fusion(f32[8192,256]{1,0:T(8,128)} %fusion.1, f32[256,256]{1,0:T(8,128)S(1)} %fusion.14, f32[1,256,8192]{2,1,0:T(8,128)} %all-gather.15.cloned.1.call-done), kind=kOutput, calls=%fused_computation.1 | convolution fusion | flops 3223322624 | bytes 25427968 | tf_op jit(solution)/shard_map/dot_general | solution.py:11
  (8 shorter events, 0.2 us)
Async XLA Ops:
  6.5 147.6 %all-gather.9.cloned.1.call-start = ((), (), s32[]{:S(2)}) async-start(), calls=%async_computation.9 | async-start | bytes 8912896 | tf_op jit(solution)/shard_map/all_gather | solution.py:29
  9.4 206.2 %all-gather.11.cloned.1.call-start = ((), (), s32[]{:S(2)}) async-start(), calls=%async_computation.10 | async-start | bytes 8912896 | tf_op jit(solution)/shard_map/all_gather | solution.py:29
  10.2 265.5 %all-gather.13.cloned.1.call-start = ((), (), s32[]{:S(2)}) async-start(), calls=%async_computation.11 | async-start | bytes 8912896 | tf_op jit(solution)/shard_map/all_gather | solution.py:29
  10.9 324.8 %all-gather.15.cloned.1.call-start = ((), (), s32[]{:S(2)}) async-start(), calls=%async_computation.12 | async-start | bytes 8912896 | tf_op jit(solution)/shard_map/all_gather | solution.py:29
  154.1 35.8 %copy-start = (f32[4,256,256]{2,1,0:T(8,128)S(1)}, f32[4,256,256]{2,1,0:T(8,128)}, u32[]{:S(2)}) copy-start(f32[4,256,256]{2,1,0:T(8,128)} %param.5) | copy-start | bytes 3145732
Sparse Core Ops, SparseCore 0:
  9.5 144.2 all-gather.8
  155.6 59.9 all-gather.10
  217.3 58.3 all-gather.12
  277.3 58.3 all-gather.14

commit v2 on v1

v2 whole, which is shorter than its diff:
```python
import functools

import jax
import jax.numpy as jnp
from jax import lax
from jax.experimental import pallas as pl
from jax.experimental.pallas import tpu as pltpu
from jax.sharding import PartitionSpec as P

HIGHEST = lax.Precision.HIGHEST
TILE = 2048
VMEM = 56 * 2**20

X_SIZE = 4


def split(values):
    high = values.astype(jnp.bfloat16)
    return high, (values - high.astype(jnp.float32)).astype(jnp.bfloat16)


def three_pass(left, right, dims):
    mul = functools.partial(
        lax.dot_general, dimension_numbers=(dims, ((), ())), preferred_element_type=jnp.float32
    )
    return mul(left[0], right[0]) + (mul(left[0], right[1]) + mul(left[1], right[0]))


def read(refs):
    return jnp.concatenate([ref[...] for ref in refs], 0)


def sums_kernel(n_late, n_early, *refs):
    vectors_ref, out_ref = refs[n_late + n_early :]
    late, early = split(read(refs[:n_late])), split(read(refs[n_late : n_late + n_early]))
    vectors = split(vectors_ref[...])
    size = late[0].shape[0]
    both = tuple(jnp.concatenate([e, l], 0) for e, l in zip(early, late))

    @pl.when(pl.program_id(0) == 0)
    def _():
        out_ref[...] = jnp.zeros_like(out_ref)

    out_ref[0 : 2 * size, :] += three_pass(both, vectors, ((1,), (0,)))
    out_ref[2 * size : 3 * size, :] += three_pass(late, early, ((1,), (1,)))


def pair_sums(late, early, vectors):
    rows, columns = vectors.shape
    size = sum(part.shape[0] for part in late)
    panels = [pl.BlockSpec((part.shape[0], TILE), lambda i: (0, i)) for part in (*late, *early)]
    return pl.pallas_call(
        functools.partial(sums_kernel, len(late), len(early)),
        grid=(rows // TILE,),
        in_specs=[*panels, pl.BlockSpec((TILE, columns), lambda i: (i, 0))],
        out_specs=pl.BlockSpec((3 * size, columns), lambda i: (0, 0)),
        out_shape=jax.ShapeDtypeStruct((3 * size, columns), jnp.float32),
        compiler_params=pltpu.CompilerParams(dimension_semantics=("arbitrary",), vmem_limit_bytes=VMEM),
        cost_estimate=pl.CostEstimate(
            flops=18 * size * rows * columns,
            bytes_accessed=4 * rows * (2 * size + columns),
            transcendentals=0,
        ),
    )(*late, *early, vectors)


def update_kernel(n_late, n_early, *refs):
    coeffs_ref, vectors_ref, out_ref = refs[n_late + n_early :]
    late, early = read(refs[:n_late]), read(refs[n_late : n_late + n_early])
    size = late.shape[0]
    dims = ((0,), (0,))
    change = three_pass(split(early), split(coeffs_ref[0:size, :]), dims)
    change += three_pass(split(late), split(coeffs_ref[size : 2 * size, :]), dims)
    out_ref[...] = vectors_ref[...] - change


def pair_update(late, early, coeffs, vectors):
    rows, columns = vectors.shape
    size = sum(part.shape[0] for part in late)
    panels = [pl.BlockSpec((part.shape[0], TILE), lambda i: (0, i)) for part in (*late, *early)]
    block = pl.BlockSpec((TILE, columns), lambda i: (i, 0))
    return pl.pallas_call(
        functools.partial(update_kernel, len(late), len(early)),
        grid=(rows // TILE,),
        in_specs=[*panels, pl.BlockSpec((2 * size, columns), lambda i: (0, 0)), block],
        out_specs=block,
        out_shape=jax.ShapeDtypeStruct((rows, columns), jnp.float32),
        compiler_params=pltpu.CompilerParams(dimension_semantics=("arbitrary",), vmem_limit_bytes=VMEM),
        cost_estimate=pl.CostEstimate(
            flops=12 * size * rows * columns,
            bytes_accessed=4 * rows * (2 * size + 2 * columns),
            transcendentals=0,
        ),
    )(*late, *early, coeffs, vectors)


def sum_rows(values, size):
    slices = values.reshape(size, values.shape[0] // size, values.shape[1])
    mine = lax.all_to_all(slices, "row", split_axis=0, concat_axis=0, tiled=True).sum(0)
    copies = jnp.broadcast_to(mine[None], slices.shape)
    return lax.all_to_all(copies, "row", split_axis=0, concat_axis=0, tiled=True).reshape(values.shape)


def exact(a, b):
    return jnp.matmul(a, b, precision=HIGHEST, preferred_element_type=jnp.float32)


def step(z, core, size):
    return [(i, (i // 8 ^ z) * 8 + i // 2 % X_SIZE * 2 + (i % 2 ^ core)) for i in range(size)]


def along_x(size):
    return [[z * 8 + x * 2 + core for x in range(X_SIZE)] for z in range(size // 8) for core in range(2)]


def along_x_and_core(size):
    return [[z * 8 + rest for rest in range(8)] for z in range(size // 8)]


def one_hot(blocks, width, size):
    column = blocks[:, None] * width + jnp.arange(width)[None]
    return (column.reshape(-1, 1) == jnp.arange(size * width)[None]).astype(jnp.float32)


def orders(width, size):
    me = lax.axis_index("col")
    z, core = me // 8, me % 2
    block = jnp.arange(size)
    late = (z + block % 2) % 2 * 8 + block // 2
    early = (z + block // 4 % 2) % 2 * 8 + block % 4 * 2 + (core + block // 8) % 2
    return one_hot(late, width, size), one_hot(early, width, size)


def gather(own, size):
    def send(value, z=0, core=0):
        return lax.ppermute(value, "col", step(z, core, size))

    even, odd = own[0::2], own[1::2]
    even_z = send(even, z=1)
    odd_x = lax.all_gather(odd, "col", axis=1, tiled=True, axis_index_groups=along_x(size))
    panels = []
    for k in reversed(range(own.shape[0] // 2)):
        both = jnp.concatenate([even[k], even_z[k]], 0)
        late = lax.all_gather(both, "col", axis=0, tiled=True, axis_index_groups=along_x_and_core(size))
        near = odd_x[k]
        far = send(near, z=1)
        panels.append(((late,), (near, far, send(near, core=1), send(far, core=1))))
    return panels


def solution(mesh):
    row_size, col_size = mesh.shape["row"], mesh.shape["col"]

    def local(band_vectors, reflectors, t_factors):
        count, _, width = reflectors.shape
        own = jnp.swapaxes(reflectors, 1, 2)
        late_order, early_order = orders(width, col_size)
        vectors = lax.all_to_all(band_vectors, "col", split_axis=1, concat_axis=0, tiled=True)
        panels = gather(own, col_size)
        for first, (late, early) in zip(range(count - 2, -1, -2), panels):
            late_t = exact(exact(late_order, t_factors[first]), late_order.T)
            early_t = exact(exact(early_order, t_factors[first + 1]), early_order.T)
            size = late_t.shape[0]
            sums = sum_rows(pair_sums(late, early, vectors), row_size)
            early_coeffs = exact(early_t, sums[:size])
            rest = sums[size : 2 * size] - exact(sums[2 * size :], early_coeffs)
            coeffs = jnp.concatenate([early_coeffs, exact(late_t, rest)], 0)
            vectors = pair_update(late, early, coeffs, vectors)
        return vectors

    in_specs = (P(("row", "col"), None), P(None, "row", "col"), P())
    return jax.shard_map(local, mesh=mesh, in_specs=in_specs, out_specs=P("row", "col"), check_vma=False)
```

time: 398 us -> 365 us (0.917); the launches traced: 393 us -> 365 us
  blocking collectives: 242 us -> 0 us
  waiting for transfers between devices: 28 us -> 221 us
  matrix products: 103 us -> 7.08 us
  Pallas kernels: 0 us -> 68.5 us
  starting transfers between devices: 0.12 us -> 33.7 us
  local copies, waits for them, and re-layouts: 7.13 us -> 16.6 us
  other arithmetic: 0.08 us -> 4.17 us
    all_to_all x9 -> x0, blocking collectives: 242 us -> none  [the longest x1 138 us: local(): lax.all_to_all(band_vectors, 'col', split_axis=1, concat_axis=0, tiled=True)]
    ppermute x0 -> x7, waiting for transfers between devices: none -> 152 us  [send(): return lax.ppermute(value, 'col', step(z, core, size))]
    dot_general x12 -> x14, matrix products: 103 us -> 7.08 us  [exact(): jnp.matmul(a, b, precision=HIGHEST, preferred_element_type=jnp.float32)]
    pallas_call x0 -> x4, Pallas kernels: none -> 68.5 us  [the longest x2 38 us: pair_sums(): pl.pallas_call(functools.partial(sums_kernel, len(late), len(early)), gri...]
    all_to_all x0 -> x5, waiting for transfers between devices: none -> 44.3 us  [the longest x2 25.7 us: sum_rows(): lax.all_to_all(copies, 'row', split_axis=0, concat_axis=0, tiled=True)]
    all_to_all x0 -> x5, starting transfers between devices: none -> 25.4 us  [the longest x2 10.8 us: sum_rows(): lax.all_to_all(slices, 'row', split_axis=0, concat_axis=0, tiled=True)]
    ppermute x0 -> x7, starting transfers between devices: none -> 8.19 us  [send(): return lax.ppermute(value, 'col', step(z, core, size))]
    squeeze x0 -> x3, local copies, waits for them, and re-layouts: none -> 4.09 us  [the longest x1 3.95 us: gather(): near = odd_x[k]]
  transfers between devices with their start and end apart: 4 -> 15, of which waited for: 3 -> 10; matrix products, arithmetic and copies ran while one was open for 21% -> 6% of each run, Pallas kernels for 0% -> 9%
where the time goes in v2:
time: 365 us
  waiting for transfers between devices  221 us (61%)
  Pallas kernels  68.5 us (19%)
  starting transfers between devices  33.7 us (9%)
  local copies, waits for them, and re-layouts  16.6 us (5%)
  between operations  13.3 us (4%)
  matrix products  7.08 us (2%)
  other arithmetic  4.17 us (1%)
    ppermute x7, waiting for transfers between devices, send(): return lax.ppermute(value, 'col', step(z, core, size))  152 us
    pallas_call x2, Pallas kernels, pair_sums(): pl.pallas_call(functools.partial(sums_kernel, len(late), len(early)), gri...  38 us
    pallas_call x2, Pallas kernels, pair_update(): pl.pallas_call(functools.partial(update_kernel, len(late), len(early)), g...  30.6 us
    all_to_all x2, waiting for transfers between devices, sum_rows(): lax.all_to_all(copies, 'row', split_axis=0, concat_axis=0, tiled=True)  25.7 us
    all_gather x1, waiting for transfers between devices, gather(): lax.all_gather(odd, 'col', axis=1, tiled=True, axis_index_groups=along_x(...  25.3 us
    all_to_all x2, waiting for transfers between devices, sum_rows(): lax.all_to_all(slices, 'row', split_axis=0, concat_axis=0, tiled=True)  16.9 us
    all_to_all x2, starting transfers between devices, sum_rows(): lax.all_to_all(slices, 'row', split_axis=0, concat_axis=0, tiled=True)  10.8 us
    ppermute x7, starting transfers between devices, send(): return lax.ppermute(value, 'col', step(z, core, size))  8.19 us
  transfers between devices with their start and end apart: 15, of which 10 were waited for; matrix products, arithmetic and copies ran while one was open for 6% of the time, Pallas kernels for 9%

profile of v2, /device:TPU:1, one launch (start us, length us, event | category | flops | bytes accessed | tf_op | source)
XLA Modules:
  0.0 364.5 jit_solution(17785317013744277679)
XLA Ops:
  6.5 2.7 fusion.46
  9.3 2.5 collective-permute-start
  11.9 22.9 %collective-permute-done = f32[2,16,8192]{2,1,0:T(8,128)S(1)} collective-permute-done((f32[2,16,8192]{2,1,0:T(8,128)S(1)}, f32[2,16,8192]{2,1,0:T(8,128)S(1)}, u32[]{:S(2)}, u32[]{:S(2)}) %collective-permute-start) | collective-permute-done | bytes 1048608 | tf_op jit(solution)/shard_map/ppermute | solution.py:136
  34.9 1.1 pad_maximum_fusion.1
  36.0 1.1 pad_maximum_fusion
  37.1 7.8 %copy.7 = f32[64,16,8,256]{3,2,0,1:T(8,128)} copy(f32[64,16,8,256]{3,2,1,0:T(8,128)} %bitcast.49) | data formatting | bytes 16777216 | tf_op jit(solution)/shard_map/all_to_all | solution.py:158
  44.9 6.6 %all-to-all-start = ((f32[512,16,256]{2,0,1:T(8,128)}), f32[512,16,256]{2,0,1:T(8,128)}, u32[]{:S(2)}, u32[]{:S(2)}) async-start(f32[512,16,256]{2,0,1:T(8,128)} %bitcast.48), calls=%async_computation | async-start | bytes 16777216 | tf_op jit(solution)/shard_map/all_to_all | solution.py:158
  51.5 25.3 %all-gather.6.cloned.1.call-done = f32[2,64,8192]{2,1,0:T(8,128)} async-done(((f32[2,16,8192]{2,1,0:T(8,128)}), f32[2,64,8192]{2,1,0:T(8,128)}) %all-gather.6.cloned.1.call-update) | async-done | bytes 4194320 | tf_op jit(solution)/shard_map/all_gather | solution.py:140
  76.8 3.9 %slice_bitcast_fusion = (f32[64,8192]{1,0:T(8,128)}, f32[64,8192]{1,0:T(8,128)S(1)}) fusion(f32[2,64,8192]{2,1,0:T(8,128)} %all-gather.6.cloned.1.call-done), kind=kLoop, calls=%fused_computation.1 | loop fusion | bytes 8388608 | tf_op jit(solution)/shard_map/squeeze | solution.py:145
  80.8 1.4 collective-permute-start.4
  82.1 1.4 collective-permute-start.5
  83.6 105.3 %collective-permute-done.4.refs_2_ = f32[64,8192]{1,0:T(8,128)} collective-permute-done((f32[64,8192]{1,0:T(8,128)}, f32[64,8192]{1,0:T(8,128)}, u32[]{:S(2)}, u32[]{:S(2)}) %collective-permute-start.4) | collective-permute-done | bytes 2097184 | tf_op jit(solution)/shard_map/ppermute | solution.py:136
  188.8 0.9 collective-permute-start.6
  189.8 1.7 all-to-all-done
  191.5 2.3 collective-permute-done.6.refs_4_
  193.8 18.9 %shard_map.37 = f32[768,256]{1,0:T(8,128)} custom-call(f32[256,8192]{1,0:T(8,128)} %all-gather.8.cloned.1.call-done.refs_0_, f32[64,8192]{1,0:T(8,128)} %get-tuple-element.5.refs_1_, f32[64,8192]{1,0:T(8,128)} %collective-permute-done.4.refs_2_, f32[64,8192]{1,0:T(8,128)} %collective-permute-done.5.refs_3_, f32[64,8192]{1,0:T(8,128)} %collective-permute-done.6.refs_4_, ...), custom_call_target="tpu_custom_call" | custom-call | flops 9663676416 | bytes 25165824 | tf_op jit(solution)/shard_map/pallas_call | solution.py:52
  212.8 7.2 %all-to-all-start.1 = ((f32[8,96,256]{2,1,0:T(8,128)}), f32[8,96,256]{2,1,0:T(8,128)S(1)}, u32[]{:S(2)}, u32[]{:S(2)}) async-start(f32[8,96,256]{2,1,0:T(8,128)} %bitcast.55), calls=%async_computation.1 | async-start | bytes 1572864 | tf_op jit(solution)/shard_map/all_to_all | solution.py:99
  220.3 1.3 fusion.10
  221.6 0.7 collective-permute-start.2
  222.3 21.1 %collective-permute-done.1.refs_2_ = f32[64,8192]{1,0:T(8,128)} collective-permute-done((f32[64,8192]{1,0:T(8,128)S(1)}, f32[64,8192]{1,0:T(8,128)}, u32[]{:S(2)}, u32[]{:S(2)}) %collective-permute-start.1) | collective-permute-done | bytes 2097184 | tf_op jit(solution)/shard_map/ppermute | solution.py:136
  243.4 1.2 collective-permute-start.3
  244.5 2.8 all-to-all-done.1
  247.4 0.9 broadcast_in_dim.4
  248.3 4.5 %all-to-all-start.2 = ((f32[8,96,256]{2,1,0:T(8,128)}), f32[8,96,256]{2,1,0:T(8,128)S(1)}, u32[]{:S(2)}, u32[]{:S(2)}) async-start(f32[8,96,256]{2,1,0:T(8,128)} %broadcast_in_dim.4), calls=%async_computation.2 | async-start | bytes 1572864 | tf_op jit(solution)/shard_map/all_to_all | solution.py:101
  252.8 0.4 fusion.20
  253.2 1.3 fusion.8
  254.5 0.4 fusion.17
  254.9 12.4 %all-to-all-done.2 = f32[8,96,256]{2,1,0:T(8,128)S(1)} async-done(((f32[8,96,256]{2,1,0:T(8,128)}), f32[8,96,256]{2,1,0:T(8,128)S(1)}, u32[]{:S(2)}, u32[]{:S(2)}) %all-to-all-start.2) | async-done | bytes 786464 | tf_op jit(solution)/shard_map/all_to_all | solution.py:101
  267.3 0.4 fusion.4
  267.7 0.4 convolution_subtract_fusion.1
  268.1 0.4 fusion.47
  268.5 0.8 pad_maximum_fusion.2.refs_5_
  269.3 15.3 %shard_map.38.refs_5_.refs_6_ = f32[8192,256]{1,0:T(8,128)} custom-call(f32[256,8192]{1,0:T(8,128)} %all-gather.8.cloned.1.call-done.refs_0_, f32[64,8192]{1,0:T(8,128)} %get-tuple-element.5.refs_1_, f32[64,8192]{1,0:T(8,128)} %collective-permute-done.4.refs_2_, f32[64,8192]{1,0:T(8,128)} %collective-permute-done.5.refs_3_, ...), custom_call_target="tpu_custom_call" | custom-call | flops 6442450944 | bytes 33554432 | tf_op jit(solution)/shard_map/pallas_call | solution.py:82
  284.6 19.0 %shard_map.39 = f32[768,256]{1,0:T(8,128)} custom-call(f32[256,8192]{1,0:T(8,128)} %all-gather.4.cloned.1.call-done.refs_0_, f32[64,8192]{1,0:T(8,128)} %copy-done, f32[64,8192]{1,0:T(8,128)} %collective-permute-done.1.refs_2_, f32[64,8192]{1,0:T(8,128)} %collective-permute-done.2.refs_3_, f32[64,8192]{1,0:T(8,128)} %collective-permute-done.3.refs_4_, ...), custom_call_target="tpu_custom_call" | custom-call | flops 9663676416 | bytes 25165824 | tf_op jit(solution)/shard_map/pallas_call | solution.py:52
  303.6 3.5 all-to-all-start.3
  307.2 0.3 fusion.12
  307.5 14.1 %all-to-all-done.3 = f32[8,96,256]{2,1,0:T(8,128)S(1)} async-done(((f32[8,96,256]{2,1,0:T(8,128)}), f32[8,96,256]{2,1,0:T(8,128)S(1)}, u32[]{:S(2)}, u32[]{:S(2)}) %all-to-all-start.3) | async-done | bytes 786464 | tf_op jit(solution)/shard_map/all_to_all | solution.py:99
  321.7 0.9 broadcast_in_dim.5
  322.7 3.5 all-to-all-start.4
  326.2 0.3 fusion.6
  326.5 0.4 fusion.21
  327.0 0.4 fusion.16
  327.4 13.3 %all-to-all-done.4 = f32[8,96,256]{2,1,0:T(8,128)S(1)} async-done(((f32[8,96,256]{2,1,0:T(8,128)}), f32[8,96,256]{2,1,0:T(8,128)S(1)}, u32[]{:S(2)}, u32[]{:S(2)}) %all-to-all-start.4) | async-done | bytes 786464 | tf_op jit(solution)/shard_map/all_to_all | solution.py:101
  340.7 0.4 fusion.1
  341.1 0.4 convolution_subtract_fusion
  341.5 0.4 fusion.48
  341.8 0.9 pad_maximum_fusion.3.refs_5_
  342.7 15.3 %shard_map.40 = f32[8192,256]{1,0:T(8,128)} custom-call(f32[256,8192]{1,0:T(8,128)} %all-gather.4.cloned.1.call-done.refs_0_, f32[64,8192]{1,0:T(8,128)} %copy-done, f32[64,8192]{1,0:T(8,128)} %collective-permute-done.1.refs_2_, f32[64,8192]{1,0:T(8,128)} %collective-permute-done.2.refs_3_, f32[64,8192]{1,0:T(8,128)} %collective-permute-done.3.refs_4_, ...), custom_call_target="tpu_custom_call" | custom-call | flops 6442450944 | bytes 33554432 | tf_op jit(solution)/shard_map/pallas_call | solution.py:82
  (25 shorter events, 0.8 us)
Async XLA Ops:
  6.5 70.3 %all-gather.6.cloned.1.call-start = ((), (), s32[]{:S(2)}) async-start(), calls=%async_computation.6 | async-start | bytes 5242880 | tf_op jit(solution)/shard_map/all_gather | solution.py:140
  9.2 184.6 %all-gather.8.cloned.1.call-start = ((), (), s32[]{:S(2)}) async-start(), calls=%async_computation.7 | async-start | bytes 9437184 | tf_op jit(solution)/shard_map/all_gather | solution.py:144
  9.3 25.5 %collective-permute-start = (f32[2,16,8192]{2,1,0:T(8,128)S(1)}, f32[2,16,8192]{2,1,0:T(8,128)S(1)}, u32[]{:S(2)}, u32[]{:S(2)}) collective-permute-start(f32[2,16,8192]{2,1,0:T(8,128)S(1)} %get-tuple-element.8), channel_id=1, source_target_pairs={{0,8},{1,9},{2,10},{3,11},{4,12},{5,13},{6,14},{7,15},{8,0},{9,1},... | collective-permute-start | bytes 3145736 | tf_op jit(solution)/shard_map/ppermute | solution.py:136
  36.0 248.6 %all-gather.4.cloned.1.call-start = ((), (), s32[]{:S(2)}) async-start(), calls=%async_computation.5 | async-start | bytes 9437184 | tf_op jit(solution)/shard_map/all_gather | solution.py:144
  44.9 146.6 %all-to-all-start = ((f32[512,16,256]{2,0,1:T(8,128)}), f32[512,16,256]{2,0,1:T(8,128)}, u32[]{:S(2)}, u32[]{:S(2)}) async-start(f32[512,16,256]{2,0,1:T(8,128)} %bitcast.48), calls=%async_computation | async-start | bytes 16777216 | tf_op jit(solution)/shard_map/all_to_all | solution.py:158
  80.8 140.8 %copy-start = (f32[64,8192]{1,0:T(8,128)}, f32[64,8192]{1,0:T(8,128)S(1)}, u32[]{:S(2)}) copy-start(f32[64,8192]{1,0:T(8,128)S(1)} %get-tuple-element.6.refs_1_) | copy-start | bytes 6291460
  80.8 108.1 %collective-permute-start.4 = (f32[64,8192]{1,0:T(8,128)}, f32[64,8192]{1,0:T(8,128)}, u32[]{:S(2)}, u32[]{:S(2)}) collective-permute-start(f32[64,8192]{1,0:T(8,128)} %get-tuple-element.5.refs_1_), channel_id=1, source_target_pairs={{0,8},{1,9},{2,10},{3,11},{4,12},{5,13},{6,14},{7,15},{8,0},{9,1},... | collective-permute-start | bytes 6291464 | tf_op jit(solution)/shard_map/ppermute | solution.py:136
  82.1 109.4 %collective-permute-start.5 = (f32[64,8192]{1,0:T(8,128)}, f32[64,8192]{1,0:T(8,128)}, u32[]{:S(2)}, u32[]{:S(2)}) collective-permute-start(f32[64,8192]{1,0:T(8,128)} %get-tuple-element.5.refs_1_), channel_id=1, source_target_pairs={{0,1},{1,0},{2,3},{3,2},{4,5},{5,4},{6,7},{7,6},{8,9},{9,8},{10,11... | collective-permute-start | bytes 6291464 | tf_op jit(solution)/shard_map/ppermute | solution.py:136
  188.8 5.0 %collective-permute-start.6 = (f32[64,8192]{1,0:T(8,128)}, f32[64,8192]{1,0:T(8,128)}, u32[]{:S(2)}, u32[]{:S(2)}) collective-permute-start(f32[64,8192]{1,0:T(8,128)} %collective-permute-done.4.refs_2_), channel_id=1, source_target_pairs={{0,1},{1,0},{2,3},{3,2},{4,5},{5,4},{6,7},{7,6},{8,9},{9,8},{10,11... | collective-permute-start | bytes 6291464 | tf_op jit(solution)/shard_map/ppermute | solution.py:136
  189.7 53.7 %collective-permute-start.1 = (f32[64,8192]{1,0:T(8,128)S(1)}, f32[64,8192]{1,0:T(8,128)}, u32[]{:S(2)}, u32[]{:S(2)}) collective-permute-start(f32[64,8192]{1,0:T(8,128)S(1)} %get-tuple-element.6.refs_1_), channel_id=1, source_target_pairs={{0,8},{1,9},{2,10},{3,11},{4,12},{5,13},{6,14},{7,15},{8,0},{9,1},... | collective-permute-start | bytes 6291464 | tf_op jit(solution)/shard_map/ppermute | solution.py:136
  212.8 34.5 %all-to-all-start.1 = ((f32[8,96,256]{2,1,0:T(8,128)}), f32[8,96,256]{2,1,0:T(8,128)S(1)}, u32[]{:S(2)}, u32[]{:S(2)}) async-start(f32[8,96,256]{2,1,0:T(8,128)} %bitcast.55), calls=%async_computation.1 | async-start | bytes 1572864 | tf_op jit(solution)/shard_map/all_to_all | solution.py:99
  221.6 63.0 %collective-permute-start.2 = (f32[64,8192]{1,0:T(8,128)S(1)}, f32[64,8192]{1,0:T(8,128)}, u32[]{:S(2)}, u32[]{:S(2)}) collective-permute-start(f32[64,8192]{1,0:T(8,128)S(1)} %get-tuple-element.6.refs_1_), channel_id=1, source_target_pairs={{0,1},{1,0},{2,3},{3,2},{4,5},{5,4},{6,7},{7,6},{8,9},{9,8},{10,11... | collective-permute-start | bytes 6291464 | tf_op jit(solution)/shard_map/ppermute | solution.py:136
  243.4 41.2 %collective-permute-start.3 = (f32[64,8192]{1,0:T(8,128)}, f32[64,8192]{1,0:T(8,128)}, u32[]{:S(2)}, u32[]{:S(2)}) collective-permute-start(f32[64,8192]{1,0:T(8,128)} %collective-permute-done.1.refs_2_), channel_id=1, source_target_pairs={{0,1},{1,0},{2,3},{3,2},{4,5},{5,4},{6,7},{7,6},{8,9},{9,8},{10,11... | collective-permute-start | bytes 6291464 | tf_op jit(solution)/shard_map/ppermute | solution.py:136
  248.3 19.0 %all-to-all-start.2 = ((f32[8,96,256]{2,1,0:T(8,128)}), f32[8,96,256]{2,1,0:T(8,128)S(1)}, u32[]{:S(2)}, u32[]{:S(2)}) async-start(f32[8,96,256]{2,1,0:T(8,128)} %broadcast_in_dim.4), calls=%async_computation.2 | async-start | bytes 1572864 | tf_op jit(solution)/shard_map/all_to_all | solution.py:101
  284.6 22.6 %copy-start.1 = (f32[4,256,256]{2,1,0:T(8,128)S(1)}, f32[4,256,256]{2,1,0:T(8,128)}, u32[]{:S(2)}) copy-start(f32[4,256,256]{2,1,0:T(8,128)} %param.5) | copy-start | bytes 3145732
  303.6 18.0 %all-to-all-start.3 = ((f32[8,96,256]{2,1,0:T(8,128)}), f32[8,96,256]{2,1,0:T(8,128)S(1)}, u32[]{:S(2)}, u32[]{:S(2)}) async-start(f32[8,96,256]{2,1,0:T(8,128)} %bitcast.56), calls=%async_computation.3 | async-start | bytes 1572864 | tf_op jit(solution)/shard_map/all_to_all | solution.py:99
  322.7 18.0 %all-to-all-start.4 = ((f32[8,96,256]{2,1,0:T(8,128)}), f32[8,96,256]{2,1,0:T(8,128)S(1)}, u32[]{:S(2)}, u32[]{:S(2)}) async-start(f32[8,96,256]{2,1,0:T(8,128)} %broadcast_in_dim.5), calls=%async_computation.4 | async-start | bytes 1572864 | tf_op jit(solution)/shard_map/all_to_all | solution.py:101
Sparse Core Ops, SparseCore 0:
  9.3 67.4 all-gather.5
  78.5 107.7 all-gather.7
  188.0 58.2 all-gather.3

commit v3 on v1

v3 whole, which is shorter than its diff:
```python
import functools

import jax
import jax.numpy as jnp
from jax import lax
from jax.experimental import pallas as pl
from jax.experimental.pallas import tpu as pltpu
from jax.sharding import PartitionSpec as P

HIGHEST = lax.Precision.HIGHEST
TILE = 1024
DEPTH = 4
VMEM = 56 * 2**20

X_SIZE = 4


def split(values):
    high = values.astype(jnp.bfloat16)
    return high, (values - high.astype(jnp.float32)).astype(jnp.bfloat16)


def three_pass(left, right, dims):
    mul = functools.partial(
        lax.dot_general, dimension_numbers=(dims, ((), ())), preferred_element_type=jnp.float32
    )
    return mul(left[0], right[0]) + (mul(left[0], right[1]) + mul(left[1], right[0]))


def read(refs):
    return jnp.concatenate([ref[...] for ref in refs], 0)


def panel_specs(parts):
    return [buffered((part.shape[0], TILE), lambda i: (0, i)) for part in parts]


def buffered(shape, index):
    return pl.BlockSpec(shape, index, pipeline_mode=pl.Buffered(DEPTH))


def sums_kernel(n_late, n_early, *refs):
    out_ref = refs[-1]
    rows, columns = refs[-2].shape
    out_ref[...] = jnp.zeros_like(out_ref)

    def body(*tiles):
        late, early = split(read(tiles[:n_late])), split(read(tiles[n_late : n_late + n_early]))
        vectors = split(tiles[-1][...])
        size = late[0].shape[0]
        both = tuple(jnp.concatenate([e, l], 0) for e, l in zip(early, late))
        out_ref[0 : 2 * size, :] += three_pass(both, vectors, ((1,), (0,)))
        out_ref[2 * size : 3 * size, :] += three_pass(late, early, ((1,), (1,)))

    pltpu.emit_pipeline(
        body,
        grid=(rows // TILE,),
        in_specs=[*panel_specs(refs[:-2]), buffered((TILE, columns), lambda i: (i, 0))],
    )(*refs[:-1])


def pair_sums(late, early, vectors):
    rows, columns = vectors.shape
    size = sum(part.shape[0] for part in late)
    anywhere = pl.BlockSpec(memory_space=pl.ANY)
    return pl.pallas_call(
        functools.partial(sums_kernel, len(late), len(early)),
        in_specs=[anywhere] * (len(late) + len(early) + 1),
        out_specs=pl.BlockSpec(memory_space=pltpu.VMEM),
        out_shape=jax.ShapeDtypeStruct((3 * size, columns), jnp.float32),
        compiler_params=pltpu.CompilerParams(vmem_limit_bytes=VMEM),
        cost_estimate=pl.CostEstimate(
            flops=18 * size * rows * columns,
            bytes_accessed=4 * rows * (2 * size + columns),
            transcendentals=0,
        ),
    )(*late, *early, vectors)


def update_kernel(n_late, n_early, *refs):
    coeffs_ref, vectors_ref, out_ref = refs[n_late + n_early :]
    rows, columns = vectors_ref.shape
    coeffs = split(coeffs_ref[...])

    def body(*tiles):
        both = split(read((*tiles[n_late : n_late + n_early], *tiles[:n_late])))
        tiles[-1][...] = tiles[-2][...] - three_pass(both, coeffs, ((0,), (0,)))

    block = buffered((TILE, columns), lambda i: (i, 0))
    pltpu.emit_pipeline(
        body,
        grid=(rows // TILE,),
        in_specs=[*panel_specs(refs[: n_late + n_early]), block],
        out_specs=[pl.BlockSpec((TILE, columns), lambda i: (i, 0))],
    )(*refs[: n_late + n_early], vectors_ref, out_ref)


def pair_update(late, early, coeffs, vectors):
    rows, columns = vectors.shape
    size = sum(part.shape[0] for part in late)
    anywhere = pl.BlockSpec(memory_space=pl.ANY)
    return pl.pallas_call(
        functools.partial(update_kernel, len(late), len(early)),
        in_specs=[
            *[anywhere] * (len(late) + len(early)),
            pl.BlockSpec(memory_space=pltpu.VMEM),
            anywhere,
        ],
        out_specs=anywhere,
        out_shape=jax.ShapeDtypeStruct((rows, columns), jnp.float32),
        compiler_params=pltpu.CompilerParams(vmem_limit_bytes=VMEM),
        cost_estimate=pl.CostEstimate(
            flops=12 * size * rows * columns,
            bytes_accessed=4 * rows * (2 * size + 2 * columns),
            transcendentals=0,
        ),
    )(*late, *early, coeffs, vectors)


def sum_rows(values, size):
    slices = values.reshape(size, values.shape[0] // size, values.shape[1])
    mine = lax.all_to_all(slices, "row", split_axis=0, concat_axis=0, tiled=True).sum(0)
    copies = jnp.broadcast_to(mine[None], slices.shape)
    sums = lax.all_to_all(copies, "row", split_axis=0, concat_axis=0, tiled=True).reshape(values.shape)
    return sums, mine


def exact(a, b):
    return jnp.matmul(a, b, precision=HIGHEST, preferred_element_type=jnp.float32)


def step(z, x, core, size):
    return [(i, (i // 8 ^ z) * 8 + (i // 2 + x) % X_SIZE * 2 + (i % 2 ^ core)) for i in range(size)]


def send(value, z=0, x=0, core=0):
    return lax.ppermute(value, "col", step(z, x, core, lax.axis_size("col")))


def gather(value, groups):
    return lax.all_gather(value, "col", axis=value.ndim - 2, tiled=True, axis_index_groups=groups)


def along_x(size):
    return [[z * 8 + x * 2 + core for x in range(X_SIZE)] for z in range(size // 8) for core in range(2)]


def along_x_and_core(size):
    return [[z * 8 + rest for rest in range(8)] for z in range(size // 8)]


def behind(value, first):
    return lax.optimization_barrier((value, first))[0]


def reorder(factor, places):
    z, x, core = (jnp.stack([jnp.asarray(place[axis]) for place in places]) for axis in range(3))
    width = factor.shape[0] // len(places)
    column = (z % 2 * 8 + x % X_SIZE * 2 + core % 2)[:, None] * width + jnp.arange(width)[None]
    pick = (column.reshape(-1, 1) == jnp.arange(factor.shape[0])[None]).astype(jnp.float32)
    return exact(exact(pick, factor), pick.T)


def apply_pair(late, early, late_t, early_t, vectors, row_size):
    size = late_t.shape[0]
    sums, mine = sum_rows(pair_sums(late, early, vectors), row_size)
    early_coeffs = exact(early_t, sums[:size])
    rest = sums[size : 2 * size] - exact(sums[2 * size :], early_coeffs)
    coeffs = jnp.concatenate([early_coeffs, exact(late_t, rest)], 0)
    return pair_update(late, early, coeffs, vectors), mine, coeffs


def solution(mesh):
    row_size, col_size = mesh.shape["row"], mesh.shape["col"]
    cat = functools.partial(jnp.concatenate, axis=0)

    def local(band_vectors, reflectors, t_factors):
        rows, width = reflectors.shape[1:]
        own = jnp.swapaxes(reflectors, 1, 2)
        me = lax.axis_index("col")
        z, x, core = me // 8, me // 2 % X_SIZE, me % 2

        near = gather(own[3], along_x(col_size))
        blocks = band_vectors.reshape(rows // col_size, col_size, -1).transpose(1, 0, 2)
        vectors = lax.all_to_all(blocks, "col", split_axis=0, concat_axis=0, tiled=True)
        vectors = vectors.reshape(rows, -1)
        other = behind(send(own[:3], z=1), blocks)

        mine = (near, send(near, z=1))
        early = (*mine, *(send(part, core=1) for part in mine))
        early_t = reorder(
            t_factors[3],
            [(z + dz, i, core + dc) for dc in (0, 1) for dz in (0, 1) for i in range(X_SIZE)],
        )
        by_z = [(z + dz, i, c) for i in range(X_SIZE) for c in (0, 1) for dz in (0, 1)]
        late = (gather(behind(cat([own[2], other[2]]), near), along_x_and_core(col_size)),)
        late_t = reorder(t_factors[2], by_z)
        first = vectors
        vectors, slice_sum, coeffs = apply_pair(late, early, late_t, early_t, vectors, row_size)

        early = (gather(behind(cat([own[1], other[1]]), near), along_x_and_core(col_size)),)
        early_t = reorder(t_factors[1], by_z)
        two = behind(cat([own[0], other[0]]), first)
        below = behind(send(two, x=1), slice_sum)
        above = behind(send(two, x=-1), slice_sum)
        across = send(below[:width], x=1), send(above[width:], x=-1)
        mine = behind(cat([two, below, above, *across]), coeffs)
        late = (mine, send(mine, core=1))
        late_t = reorder(
            t_factors[0],
            [(z + dz, x + dx, core + dc) for dc in (0, 1) for dx in (0, -1, 1, 2) for dz in (0, 1)],
        )
        vectors, _, _ = apply_pair(late, early, late_t, early_t, vectors, row_size)
        return vectors

    in_specs = (P(("row", "col"), None), P(None, "row", "col"), P())
    return jax.shard_map(local, mesh=mesh, in_specs=in_specs, out_specs=P("row", "col"), check_vma=False)
```

time: 398 us -> 355 us (0.89)
  blocking collectives: 242 us -> 0 us
  waiting for transfers between devices: 28 us -> 212 us
  matrix products: 103 us -> 5.19 us
  Pallas kernels: 0 us -> 55.3 us
  starting transfers between devices: 0.12 us -> 42.2 us
  local copies, waits for them, and re-layouts: 7.13 us -> 22.9 us
    all_to_all x9 -> x0, blocking collectives: 242 us -> none  [the longest x1 138 us: local(): lax.all_to_all(band_vectors, 'col', split_axis=1, concat_axis=0, tiled=True)]
    ppermute x0 -> x9, waiting for transfers between devices: none -> 169 us  [send(): return lax.ppermute(value, 'col', step(z, x, core, lax.axis_size('col')))]
    dot_general x12 -> x14, matrix products: 103 us -> 5.19 us  [exact(): jnp.matmul(a, b, precision=HIGHEST, preferred_element_type=jnp.float32)]
    pallas_call x0 -> x4, Pallas kernels: none -> 55.3 us  [the longest x2 28.3 us: pair_sums(): pl.pallas_call(functools.partial(sums_kernel, len(late), len(early)), in_...]
    all_to_all x0 -> x5, waiting for transfers between devices: none -> 42.6 us  [the longest x2 27.5 us: sum_rows(): lax.all_to_all(slices, 'row', split_axis=0, concat_axis=0, tiled=True)]
    all_to_all x0 -> x5, starting transfers between devices: none -> 29 us  [the longest x2 15 us: sum_rows(): lax.all_to_all(slices, 'row', split_axis=0, concat_axis=0, tiled=True)]
    all_gather x4 -> x3, waiting for transfers between devices: 26.1 us -> 0.01 us  [gather(): lax.all_gather(value, 'col', axis=value.ndim - 2, tiled=True, axis_index_...]
    ppermute x0 -> x9, starting transfers between devices: none -> 13.1 us  [send(): return lax.ppermute(value, 'col', step(z, x, core, lax.axis_size('col')))]
  transfers between devices with their start and end apart: 4 -> 17, of which waited for: 3 -> 9; matrix products, arithmetic and copies ran while one was open for 21% -> 7% of each run, Pallas kernels for 0% -> 8%
where the time goes in v3:
time: 355 us; the launch traced here: 354 us
  waiting for transfers between devices  212 us (60%)
  Pallas kernels  55.3 us (16%)
  starting transfers between devices  42.2 us (12%)
  local copies, waits for them, and re-layouts  22.9 us (6%)
  between operations  13.4 us (4%)
  matrix products  5.19 us (1%)
  other arithmetic  3.66 us (1%)
    ppermute x9, waiting for transfers between devices, send(): return lax.ppermute(value, 'col', step(z, x, core, lax.axis_size('col')))  169 us
    pallas_call x2, Pallas kernels, pair_sums(): pl.pallas_call(functools.partial(sums_kernel, len(late), len(early)), in_...  28.3 us
    all_to_all x2, waiting for transfers between devices, sum_rows(): lax.all_to_all(slices, 'row', split_axis=0, concat_axis=0, tiled=True)  27.5 us
    pallas_call x2, Pallas kernels, pair_update(): pl.pallas_call(functools.partial(update_kernel, len(late), len(early)), i...  26.9 us
    all_to_all x2, starting transfers between devices, sum_rows(): lax.all_to_all(slices, 'row', split_axis=0, concat_axis=0, tiled=True)  15 us
    all_to_all x2, waiting for transfers between devices, sum_rows(): lax.all_to_all(copies, 'row', split_axis=0, concat_axis=0, tiled=True)  13.3 us
    ppermute x9, starting transfers between devices, send(): return lax.ppermute(value, 'col', step(z, x, core, lax.axis_size('col')))  13.1 us
    reshape x1, local copies, waits for them, and re-layouts, local(): band_vectors.reshape(rows // col_size, col_size, -1).transpose(1, 0, 2)  7.75 us
  transfers between devices with their start and end apart: 17, of which 9 were waited for; matrix products, arithmetic and copies ran while one was open for 7% of the time, Pallas kernels for 8%

profile of v3, /device:TPU:1, one launch (start us, length us, event | category | flops | bytes accessed | tf_op | source)
XLA Modules:
  0.0 354.3 jit_solution(4930944286457768128)
XLA Ops:
  6.5 2.8 slice.81
  9.4 2.5 collective-permute-start
  11.9 1.1 slice_bitcast_fusion
  13.1 7.7 %copy.7 = f32[64,16,8,256]{3,2,0,1:T(8,128)} copy(f32[64,16,8,256]{3,2,1,0:T(8,128)} %bitcast.59) | data formatting | bytes 16777216 | tf_op jit(solution)/shard_map/reshape | solution.py:184
  20.8 25.4 %collective-permute-done = f32[3,16,8192]{2,1,0:T(8,128)} collective-permute-done((f32[3,16,8192]{2,1,0:T(8,128)}, f32[3,16,8192]{2,1,0:T(8,128)}, u32[]{:S(2)}, u32[]{:S(2)}) %collective-permute-start) | collective-permute-done | bytes 1572896 | tf_op jit(solution)/shard_map/ppermute | solution.py:137
  46.3 1.5 slice_bitcast_fusion.3
  47.7 1.5 pad_maximum_fusion.1
  49.3 6.9 %all-to-all-start = ((f32[16,512,256]{2,1,0:T(8,128)}), f32[16,512,256]{2,1,0:T(8,128)}, u32[]{:S(2)}, u32[]{:S(2)}) async-start(f32[16,512,256]{2,1,0:T(8,128)} %bitcast.58), calls=%async_computation | async-start | bytes 16777216 | tf_op jit(solution)/shard_map/all_to_all | solution.py:185
  56.3 1.5 collective-permute-start.2
  58.3 0.7 collective-permute-start.3
  59.0 134.5 %collective-permute-done.2.refs_2_ = f32[64,8192]{1,0:T(8,128)} collective-permute-done((f32[64,8192]{1,0:T(8,128)}, f32[64,8192]{1,0:T(8,128)}, u32[]{:S(2)}, u32[]{:S(2)}) %collective-permute-start.2) | collective-permute-done | bytes 2097184 | tf_op jit(solution)/shard_map/ppermute | solution.py:137
  193.5 0.9 collective-permute-start.4
  195.0 0.4 fusion.21
  195.8 0.4 fusion.19
  196.3 1.8 all-to-all-done
  198.0 2.2 collective-permute-start.1
  200.2 0.5 collective-permute-start.5
  200.7 14.2 %shard_map.37 = f32[768,256]{1,0:T(8,128)} custom-call(f32[256,8192]{1,0:T(8,128)} %all-gather.5.cloned.1.call-done.refs_0_, f32[64,8192]{1,0:T(8,128)} %bitcast.7.refs_1_, f32[64,8192]{1,0:T(8,128)} %collective-permute-done.2.refs_2_, f32[64,8192]{1,0:T(8,128)} %collective-permute-done.3.refs_3_, f32[64,8192]{1,0:T(8,128)} %collective-permute-done.4.refs_4_, ...), custom_call_target="tpu_custom_call" | custom-call | flops 9663676416 | bytes 25165824 | tf_op jit(solution)/shard_map/pallas_call | solution.py:66
  214.9 7.7 %all-to-all-start.1 = ((f32[8,96,256]{2,1,0:T(8,128)}), f32[8,96,256]{2,1,0:T(8,128)S(1)}, u32[]{:S(2)}, u32[]{:S(2)}) async-start(f32[8,96,256]{2,1,0:T(8,128)} %bitcast.67), calls=%async_computation.1 | async-start | bytes 1572864 | tf_op jit(solution)/shard_map/all_to_all | solution.py:122
  222.6 1.1 constant_dynamic-update-slice_fusion.4
  223.6 13.4 %all-to-all-done.1 = f32[8,96,256]{2,1,0:T(8,128)S(1)} async-done(((f32[8,96,256]{2,1,0:T(8,128)}), f32[8,96,256]{2,1,0:T(8,128)S(1)}, u32[]{:S(2)}, u32[]{:S(2)}) %all-to-all-start.1) | async-done | bytes 786464 | tf_op jit(solution)/shard_map/all_to_all | solution.py:122
  237.1 0.9 broadcast_in_dim.4
  238.1 3.5 %all-to-all-start.2 = ((f32[8,96,256]{2,1,0:T(8,128)}), f32[8,96,256]{2,1,0:T(8,128)S(1)}, u32[]{:S(2)}, u32[]{:S(2)}) async-start(f32[8,96,256]{2,1,0:T(8,128)} %broadcast_in_dim.4), calls=%async_computation.2 | async-start | bytes 1572864 | tf_op jit(solution)/shard_map/all_to_all | solution.py:124
  241.6 1.4 collective-permute-done.1
  243.0 2.3 collective-permute-start.6
  245.3 1.1 slice.67
  246.4 0.5 collective-permute-start.7
  246.9 1.0 constant_dynamic-update-slice_fusion.3
  248.0 2.3 constant_dynamic-update-slice_fusion.2
  250.2 6.6 %collective-permute-done.6 = f32[16,8192]{1,0:T(8,128)S(1)} collective-permute-done((f32[16,8192]{1,0:T(8,128)S(1)}, f32[16,8192]{1,0:T(8,128)S(1)}, u32[]{:S(2)}, u32[]{:S(2)}) %collective-permute-start.6) | collective-permute-done | bytes 524320 | tf_op jit(solution)/shard_map/ppermute | solution.py:137
  256.9 0.8 constant_dynamic-update-slice_fusion.1
  257.7 1.0 collective-permute-done.7
  258.7 0.9 constant_dynamic-update-slice_fusion.refs_0_
  260.7 0.8 pad_maximum_fusion.3.refs_5_
  261.6 2.1 collective-permute-start.8
  263.6 13.5 %shard_map.38.refs_3_.refs_4_ = f32[8192,256]{1,0:T(8,128)} custom-call(f32[256,8192]{1,0:T(8,128)} %all-gather.5.cloned.1.call-done.refs_0_, f32[64,8192]{1,0:T(8,128)} %bitcast.7.refs_1_, f32[64,8192]{1,0:T(8,128)} %collective-permute-done.2.refs_2_, f32[64,8192]{1,0:T(8,128)} %collective-permute-done.3.refs_3_, ...), custom_call_target="tpu_custom_call" | custom-call | flops 6442450944 | bytes 33554432 | tf_op jit(solution)/shard_map/pallas_call | solution.py:102
  277.1 14.2 %shard_map.39 = f32[768,256]{1,0:T(8,128)} custom-call(f32[128,8192]{1,0:T(8,128)} %constant_dynamic-update-slice_fusion.refs_0_, f32[128,8192]{1,0:T(8,128)} %collective-permute-done.8.refs_1_, f32[256,8192]{1,0:T(8,128)} %all-gather.7.cloned.1.call-done.refs_2_, f32[8192,256]{1,0:T(8,128)} %shard_map.38.refs_3_.refs_4_), custom_call_target="tpu_custom_call" | custom-call | flops 9663676416 | bytes 25165824 | tf_op jit(solution)/shard_map/pallas_call | solution.py:66
  291.3 7.4 %all-to-all-start.3 = ((f32[8,96,256]{2,1,0:T(8,128)}), f32[8,96,256]{2,1,0:T(8,128)S(1)}, u32[]{:S(2)}, u32[]{:S(2)}) async-start(f32[8,96,256]{2,1,0:T(8,128)} %bitcast.66), calls=%async_computation.3 | async-start | bytes 1572864 | tf_op jit(solution)/shard_map/all_to_all | solution.py:122
  299.1 14.1 %all-to-all-done.3 = f32[8,96,256]{2,1,0:T(8,128)S(1)} async-done(((f32[8,96,256]{2,1,0:T(8,128)}), f32[8,96,256]{2,1,0:T(8,128)S(1)}, u32[]{:S(2)}, u32[]{:S(2)}) %all-to-all-start.3) | async-done | bytes 786464 | tf_op jit(solution)/shard_map/all_to_all | solution.py:122
  313.3 0.9 broadcast_in_dim.5
  314.2 3.5 %all-to-all-start.4 = ((f32[8,96,256]{2,1,0:T(8,128)}), f32[8,96,256]{2,1,0:T(8,128)S(1)}, u32[]{:S(2)}, u32[]{:S(2)}) async-start(f32[8,96,256]{2,1,0:T(8,128)} %broadcast_in_dim.5), calls=%async_computation.4 | async-start | bytes 1572864 | tf_op jit(solution)/shard_map/all_to_all | solution.py:124
  317.8 0.4 fusion.18
  318.5 0.4 fusion.15
  319.0 13.3 %all-to-all-done.4 = f32[8,96,256]{2,1,0:T(8,128)S(1)} async-done(((f32[8,96,256]{2,1,0:T(8,128)}), f32[8,96,256]{2,1,0:T(8,128)S(1)}, u32[]{:S(2)}, u32[]{:S(2)}) %all-to-all-start.4) | async-done | bytes 786464 | tf_op jit(solution)/shard_map/all_to_all | solution.py:124
  332.3 0.4 fusion.1
  332.7 0.4 convolution_subtract_fusion
  333.4 0.9 pad_maximum_fusion.4.refs_3_
  334.3 13.5 %shard_map.40 = f32[8192,256]{1,0:T(8,128)} custom-call(f32[128,8192]{1,0:T(8,128)} %constant_dynamic-update-slice_fusion.refs_0_, f32[128,8192]{1,0:T(8,128)} %collective-permute-done.8.refs_1_, f32[256,8192]{1,0:T(8,128)} %all-gather.7.cloned.1.call-done.refs_2_, f32[512,256]{1,0:T(8,128)} %pad_maximum_fusion.4.refs_3_, f32[8192,256]{1,0:T(8,128)} %shard_map.38.refs_3_.refs_4_), custom_call_target="tpu_custom_call" | custom-call | flops 6442450944 | bytes 33554432 | tf_op jit(solution)/shard_map/pallas_call | solution.py:102
  (50 shorter events, 4.0 us)
Async XLA Ops:
  6.5 5.3 %copy-start = (f32[4,8192,16]{1,2,0:T(8,128)S(1)}, f32[4,8192,16]{1,2,0:T(8,128)}, u32[]{:S(2)}) copy-start(f32[4,8192,16]{1,2,0:T(8,128)} %param.4) | copy-start | bytes 6291460
  6.5 42.7 %all-gather.9.cloned.1.call-start = ((), (), s32[]{:S(2)}) async-start(), calls=%async_computation.7 | async-start | bytes 2621440 | tf_op jit(solution)/shard_map/all_gather | solution.py:141
  9.4 36.9 %collective-permute-start = (f32[3,16,8192]{2,1,0:T(8,128)}, f32[3,16,8192]{2,1,0:T(8,128)}, u32[]{:S(2)}, u32[]{:S(2)}) collective-permute-start(f32[3,16,8192]{2,1,0:T(8,128)} %slice.81), channel_id=1, source_target_pairs={{0,8},{1,9},{2,10},{3,11},{4,12},{5,13},{6,14},{7,15},{8,0},{9,1},... | collective-permute-start | bytes 4718600 | tf_op jit(solution)/shard_map/ppermute | solution.py:137
  13.0 187.7 %all-gather.5.cloned.1.call-start = ((), (), s32[]{:S(2)}) async-start(), calls=%async_computation.5 | async-start | bytes 9437184 | tf_op jit(solution)/shard_map/all_gather | solution.py:141
  13.1 34.7 %copy-start.1 = (f32[16,8192]{1,0:T(8,128)S(1)}, f32[16,8192]{1,0:T(8,128)}, u32[]{:S(2)}) copy-start(f32[16,8192]{1,0:T(8,128)} %get-tuple-element.24) | copy-start | bytes 1572868
  49.3 8.9 %copy-start.4 = (s32[16]{0:T(128)S(1)}, s32[16]{0:T(128)}, u32[]{:S(2)}) copy-start(s32[16]{0:T(128)} %constant.141.clone.1) | copy-start | bytes 196
  49.3 8.9 %copy-start.5 = (s32[16]{0:T(128)S(1)}, s32[16]{0:T(128)}, u32[]{:S(2)}) copy-start(s32[16]{0:T(128)} %constant.143.clone.1) | copy-start | bytes 196
  49.3 145.4 %copy-start.2 = (f32[4,256,256]{2,1,0:T(8,128)S(1)}, f32[4,256,256]{2,1,0:T(8,128)}, u32[]{:S(2)}) copy-start(f32[4,256,256]{2,1,0:T(8,128)} %param.5) | copy-start | bytes 3145732
  49.3 148.7 %all-to-all-start = ((f32[16,512,256]{2,1,0:T(8,128)}), f32[16,512,256]{2,1,0:T(8,128)}, u32[]{:S(2)}, u32[]{:S(2)}) async-start(f32[16,512,256]{2,1,0:T(8,128)} %bitcast.58), calls=%async_computation | async-start | bytes 16777216 | tf_op jit(solution)/shard_map/all_to_all | solution.py:185
  56.2 220.9 %all-gather.7.cloned.1.call-start = ((), (), s32[]{:S(2)}) async-start(), calls=%async_computation.6 | async-start | bytes 9437184 | tf_op jit(solution)/shard_map/all_gather | solution.py:141
  56.3 137.2 %collective-permute-start.2 = (f32[64,8192]{1,0:T(8,128)}, f32[64,8192]{1,0:T(8,128)}, u32[]{:S(2)}, u32[]{:S(2)}) collective-permute-start(f32[64,8192]{1,0:T(8,128)} %bitcast.7.refs_1_), channel_id=1, source_target_pairs={{0,8},{1,9},{2,10},{3,11},{4,12},{5,13},{6,14},{7,15},{8,0},{9,1},... | collective-permute-start | bytes 6291464 | tf_op jit(solution)/shard_map/ppermute | solution.py:137
  58.3 142.4 %collective-permute-start.3 = (f32[64,8192]{1,0:T(8,128)}, f32[64,8192]{1,0:T(8,128)}, u32[]{:S(2)}, u32[]{:S(2)}) collective-permute-start(f32[64,8192]{1,0:T(8,128)} %bitcast.7.refs_1_), channel_id=1, source_target_pairs={{0,1},{1,0},{2,3},{3,2},{4,5},{5,4},{6,7},{7,6},{8,9},{9,8},{10,11... | collective-permute-start | bytes 6291464 | tf_op jit(solution)/shard_map/ppermute | solution.py:137
  193.5 7.2 %collective-permute-start.4 = (f32[64,8192]{1,0:T(8,128)}, f32[64,8192]{1,0:T(8,128)}, u32[]{:S(2)}, u32[]{:S(2)}) collective-permute-start(f32[64,8192]{1,0:T(8,128)} %collective-permute-done.2.refs_2_), channel_id=1, source_target_pairs={{0,1},{1,0},{2,3},{3,2},{4,5},{5,4},{6,7},{7,6},{8,9},{9,8},{10,11... | collective-permute-start | bytes 6291464 | tf_op jit(solution)/shard_map/ppermute | solution.py:137
  198.0 45.0 %collective-permute-start.1 = (f32[32,8192]{1,0:T(8,128)S(1)}, f32[32,8192]{1,0:T(8,128)S(1)}, u32[]{:S(2)}, u32[]{:S(2)}) collective-permute-start(f32[32,8192]{1,0:T(8,128)S(1)} %pad_maximum_fusion), channel_id=1, source_target_pairs={{0,2},{1,3},{2,4},{3,5},{4,6},{5,7},{6,0},{7,1},{8,10},{9,11},{10,... | collective-permute-start | bytes 3145736 | tf_op jit(solution)/shard_map/ppermute | solution.py:137
  200.2 42.8 %collective-permute-start.5 = (f32[32,8192]{1,0:T(8,128)S(1)}, f32[32,8192]{1,0:T(8,128)}, u32[]{:S(2)}, u32[]{:S(2)}) collective-permute-start(f32[32,8192]{1,0:T(8,128)S(1)} %pad_maximum_fusion), channel_id=1, source_target_pairs={{0,6},{1,7},{2,0},{3,1},{4,2},{5,3},{6,4},{7,5},{8,14},{9,15},{10,... | collective-permute-start | bytes 3145736 | tf_op jit(solution)/shard_map/ppermute | solution.py:137
  214.9 22.2 %all-to-all-start.1 = ((f32[8,96,256]{2,1,0:T(8,128)}), f32[8,96,256]{2,1,0:T(8,128)S(1)}, u32[]{:S(2)}, u32[]{:S(2)}) async-start(f32[8,96,256]{2,1,0:T(8,128)} %bitcast.67), calls=%async_computation.1 | async-start | bytes 1572864 | tf_op jit(solution)/shard_map/all_to_all | solution.py:122
  238.1 21.5 %all-to-all-start.2 = ((f32[8,96,256]{2,1,0:T(8,128)}), f32[8,96,256]{2,1,0:T(8,128)S(1)}, u32[]{:S(2)}, u32[]{:S(2)}) async-start(f32[8,96,256]{2,1,0:T(8,128)} %broadcast_in_dim.4), calls=%async_computation.2 | async-start | bytes 1572864 | tf_op jit(solution)/shard_map/all_to_all | solution.py:124
  243.0 13.8 %collective-permute-start.6 = (f32[16,8192]{1,0:T(8,128)S(1)}, f32[16,8192]{1,0:T(8,128)S(1)}, u32[]{:S(2)}, u32[]{:S(2)}) collective-permute-start(f32[16,8192]{1,0:T(8,128)S(1)} %slice.66), channel_id=1, source_target_pairs={{0,2},{1,3},{2,4},{3,5},{4,6},{5,7},{6,0},{7,1},{8,10},{9,11},{10,... | collective-permute-start | bytes 1572872 | tf_op jit(solution)/shard_map/ppermute | solution.py:137
  246.4 12.3 %collective-permute-start.7 = (f32[16,8192]{1,0:T(8,128)S(1)}, f32[16,8192]{1,0:T(8,128)S(1)}, u32[]{:S(2)}, u32[]{:S(2)}) collective-permute-start(f32[16,8192]{1,0:T(8,128)S(1)} %slice.67), channel_id=1, source_target_pairs={{0,6},{1,7},{2,0},{3,1},{4,2},{5,3},{6,4},{7,5},{8,14},{9,15},{10,... | collective-permute-start | bytes 1572872 | tf_op jit(solution)/shard_map/ppermute | solution.py:137
  261.6 15.5 %collective-permute-start.8 = (f32[128,8192]{1,0:T(8,128)}, f32[128,8192]{1,0:T(8,128)}, u32[]{:S(2)}, u32[]{:S(2)}) collective-permute-start(f32[128,8192]{1,0:T(8,128)} %constant_dynamic-update-slice_fusion.refs_0_), channel_id=1, source_target_pairs={{0,1},{1,0},{2,3},{3,2},{4,5},{5,4},{6,7},{7,6},{8,9},{9,8},{10,11... | collective-permute-start | bytes 12582920 | tf_op jit(solution)/shard_map/ppermute | solution.py:137
  277.1 21.7 %copy-start.3 = (f32[4,256,256]{2,1,0:T(8,128)S(1)}, f32[4,256,256]{2,1,0:T(8,128)}, u32[]{:S(2)}) copy-start(f32[4,256,256]{2,1,0:T(8,128)} %param.5) | copy-start | bytes 3145732
  291.3 22.0 %all-to-all-start.3 = ((f32[8,96,256]{2,1,0:T(8,128)}), f32[8,96,256]{2,1,0:T(8,128)S(1)}, u32[]{:S(2)}, u32[]{:S(2)}) async-start(f32[8,96,256]{2,1,0:T(8,128)} %bitcast.66), calls=%async_computation.3 | async-start | bytes 1572864 | tf_op jit(solution)/shard_map/all_to_all | solution.py:122
  314.2 18.0 %all-to-all-start.4 = ((f32[8,96,256]{2,1,0:T(8,128)}), f32[8,96,256]{2,1,0:T(8,128)S(1)}, u32[]{:S(2)}, u32[]{:S(2)}) async-start(f32[8,96,256]{2,1,0:T(8,128)} %broadcast_in_dim.5), calls=%async_computation.4 | async-start | bytes 1572864 | tf_op jit(solution)/shard_map/all_to_all | solution.py:124
Sparse Core Ops, SparseCore 0:
  13.1 32.9 all-gather.8
  49.4 114.3 all-gather.4
  165.5 75.3 all-gather.6

commit v4 on v3

--- a/solution.py
+++ b/solution.py
@@ -39,8 +39,26 @@
     return pl.BlockSpec(shape, index, pipeline_mode=pl.Buffered(DEPTH))
 
 
-def sums_kernel(n_late, n_early, *refs):
+def views(refs, parts):
+    return [ref if index is None else ref.at[index] for ref, (_, index) in zip(refs, parts)]
+
+
+def arrays(parts):
+    return [array for array, _ in parts]
+
+
+def shapes(parts):
+    return tuple((array.shape, index) for array, index in parts)
+
+
+def height(parts):
+    return sum(array.shape[-2] for array, _ in parts)
+
+
+def sums_kernel(late, early, *refs):
+    n_late, n_early = len(late), len(early)
     out_ref = refs[-1]
+    panels = views(refs, late + early)
     rows, columns = refs[-2].shape
     out_ref[...] = jnp.zeros_like(out_ref)
 
@@ -55,16 +73,16 @@
     pltpu.emit_pipeline(
         body,
         grid=(rows // TILE,),
-        in_specs=[*panel_specs(refs[:-2]), buffered((TILE, columns), lambda i: (i, 0))],
-    )(*refs[:-1])
+        in_specs=[*panel_specs(panels), buffered((TILE, columns), lambda i: (i, 0))],
+    )(*panels, refs[-2])
 
 
 def pair_sums(late, early, vectors):
     rows, columns = vectors.shape
-    size = sum(part.shape[0] for part in late)
+    size = height(late)
     anywhere = pl.BlockSpec(memory_space=pl.ANY)
     return pl.pallas_call(
-        functools.partial(sums_kernel, len(late), len(early)),
+        functools.partial(sums_kernel, shapes(late), shapes(early)),
         in_specs=[anywhere] * (len(late) + len(early) + 1),
         out_specs=pl.BlockSpec(memory_space=pltpu.VMEM),
         out_shape=jax.ShapeDtypeStruct((3 * size, columns), jnp.float32),
@@ -74,10 +92,12 @@
             bytes_accessed=4 * rows * (2 * size + columns),
             transcendentals=0,
         ),
-    )(*late, *early, vectors)
-
-
-def update_kernel(n_late, n_early, *refs):
+    )(*arrays(late + early), vectors)
+
+
+def update_kernel(late, early, *refs):
+    n_late, n_early = len(late), len(early)
+    panels = views(refs, late + early)
     coeffs_ref, vectors_ref, out_ref = refs[n_late + n_early :]
     rows, columns = vectors_ref.shape
     coeffs = split(coeffs_ref[...])
@@ -90,17 +110,17 @@
     pltpu.emit_pipeline(
         body,
         grid=(rows // TILE,),
-        in_specs=[*panel_specs(refs[: n_late + n_early]), block],
+        in_specs=[*panel_specs(panels), block],
         out_specs=[pl.BlockSpec((TILE, columns), lambda i: (i, 0))],
-    )(*refs[: n_late + n_early], vectors_ref, out_ref)
+    )(*panels, vectors_ref, out_ref)
 
 
 def pair_update(late, early, coeffs, vectors):
     rows, columns = vectors.shape
-    size = sum(part.shape[0] for part in late)
+    size = height(late)
     anywhere = pl.BlockSpec(memory_space=pl.ANY)
     return pl.pallas_call(
-        functools.partial(update_kernel, len(late), len(early)),
+        functools.partial(update_kernel, shapes(late), shapes(early)),
         in_specs=[
             *[anywhere] * (len(late) + len(early)),
             pl.BlockSpec(memory_space=pltpu.VMEM),
@@ -114,15 +134,14 @@
             bytes_accessed=4 * rows * (2 * size + 2 * columns),
             transcendentals=0,
         ),
-    )(*late, *early, coeffs, vectors)
+    )(*arrays(late + early), coeffs, vectors)
 
 
 def sum_rows(values, size):
     slices = values.reshape(size, values.shape[0] // size, values.shape[1])
     mine = lax.all_to_all(slices, "row", split_axis=0, concat_axis=0, tiled=True).sum(0)
     copies = jnp.broadcast_to(mine[None], slices.shape)
-    sums = lax.all_to_all(copies, "row", split_axis=0, concat_axis=0, tiled=True).reshape(values.shape)
-    return sums, mine
+    return lax.all_to_all(copies, "row", split_axis=0, concat_axis=0, tiled=True).reshape(values.shape)
 
 
 def exact(a, b):
@@ -139,10 +158,6 @@
 
 def gather(value, groups):
     return lax.all_gather(value, "col", axis=value.ndim - 2, tiled=True, axis_index_groups=groups)
-
-
-def along_x(size):
-    return [[z * 8 + x * 2 + core for x in range(X_SIZE)] for z in range(size // 8) for core in range(2)]
 
 
 def along_x_and_core(size):
@@ -163,11 +178,11 @@
 
 def apply_pair(late, early, late_t, early_t, vectors, row_size):
     size = late_t.shape[0]
-    sums, mine = sum_rows(pair_sums(late, early, vectors), row_size)
+    sums = sum_rows(pair_sums(late, early, vectors), row_size)
     early_coeffs = exact(early_t, sums[:size])
     rest = sums[size : 2 * size] - exact(sums[2 * size :], early_coeffs)
     coeffs = jnp.concatenate([early_coeffs, exact(late_t, rest)], 0)
-    return pair_update(late, early, coeffs, vectors), mine, coeffs
+    return pair_update(late, early, coeffs, vectors)
 
 
 def solution(mesh):
@@ -180,38 +195,29 @@
         me = lax.axis_index("col")
         z, x, core = me // 8, me // 2 % X_SIZE, me % 2
 
-        near = gather(own[3], along_x(col_size))
+        near = gather(own[3], along_x_and_core(col_size))
         blocks = band_vectors.reshape(rows // col_size, col_size, -1).transpose(1, 0, 2)
         vectors = lax.all_to_all(blocks, "col", split_axis=0, concat_axis=0, tiled=True)
         vectors = vectors.reshape(rows, -1)
         other = behind(send(own[:3], z=1), blocks)
 
-        mine = (near, send(near, z=1))
-        early = (*mine, *(send(part, core=1) for part in mine))
+        blocks_x = near.reshape(X_SIZE, 2, width, rows)
+        far = send(lax.dynamic_index_in_dim(blocks_x, core, 1, False).reshape(-1, rows), z=1)
+        early = ((near, None), (far, None), (send(far, core=1), None))
         early_t = reorder(
             t_factors[3],
-            [(z + dz, i, core + dc) for dc in (0, 1) for dz in (0, 1) for i in range(X_SIZE)],
+            [(z, i, c) for i in range(X_SIZE) for c in (0, 1)]
+            + [(z + 1, i, core + dc) for dc in (0, 1) for i in range(X_SIZE)],
         )
+        late = ((gather(behind(cat([own[2], other[2]]), near), along_x_and_core(col_size)), None),)
         by_z = [(z + dz, i, c) for i in range(X_SIZE) for c in (0, 1) for dz in (0, 1)]
-        late = (gather(behind(cat([own[2], other[2]]), near), along_x_and_core(col_size)),)
         late_t = reorder(t_factors[2], by_z)
-        first = vectors
-        vectors, slice_sum, coeffs = apply_pair(late, early, late_t, early_t, vectors, row_size)
-
-        early = (gather(behind(cat([own[1], other[1]]), near), along_x_and_core(col_size)),)
-        early_t = reorder(t_factors[1], by_z)
-        two = behind(cat([own[0], other[0]]), first)
-        below = behind(send(two, x=1), slice_sum)
-        above = behind(send(two, x=-1), slice_sum)
-        across = send(below[:width], x=1), send(above[width:], x=-1)
-        mine = behind(cat([two, below, above, *across]), coeffs)
-        late = (mine, send(mine, core=1))
-        late_t = reorder(
-            t_factors[0],
-            [(z + dz, x + dx, core + dc) for dc in (0, 1) for dx in (0, -1, 1, 2) for dz in (0, 1)],
-        )
-        vectors, _, _ = apply_pair(late, early, late_t, early_t, vectors, row_size)
-        return vectors
+        vectors = apply_pair(late, early, late_t, early_t, vectors, row_size)
+
+        both = jnp.concatenate([own[:2], other[:2]], 1)
+        panels = gather(behind(both, near), along_x_and_core(col_size))
+        late_t, early_t = reorder(t_factors[0], by_z), reorder(t_factors[1], by_z)
+        return apply_pair(((panels, 0),), ((panels, 1),), late_t, early_t, vectors, row_size)
 
     in_specs = (P(("row", "col"), None), P(None, "row", "col"), P())
     return jax.shard_map(local, mesh=mesh, in_specs=in_specs, out_specs=P("row", "col"), check_vma=False)

time: 355 us -> 344 us (0.969)
  starting transfers between devices: 42.2 us -> 29.7 us
  local copies, waits for them, and re-layouts: 22.9 us -> 16.5 us
  waiting for transfers between devices: 212 us -> 218 us
    all_to_all x2, waiting for transfers between devices: 13.3 us -> 26.4 us  [sum_rows(): lax.all_to_all(copies, 'row', split_axis=0, concat_axis=0, tiled=True)]
    ppermute x9 -> x3, starting transfers between devices: 13.1 us -> 4.78 us  [send(): return lax.ppermute(value, 'col', step(z, x, core, lax.axis_size('col')))]
    ppermute x9 -> x3, waiting for transfers between devices: 169 us -> 162 us  [send(): return lax.ppermute(value, 'col', step(z, x, core, lax.axis_size('col')))]
    all_to_all x2, starting transfers between devices: 15 us -> 10.8 us  [sum_rows(): lax.all_to_all(slices, 'row', split_axis=0, concat_axis=0, tiled=True)]
    unnamed x16 -> x12, local copies, waits for them, and re-layouts: 5.24 us -> 1.19 us
  transfers between devices with their start and end apart: 17 -> 11, of which waited for: 9 -> 8; matrix products, arithmetic and copies ran while one was open for 7% -> 6% of each run, Pallas kernels for 8% -> 8%
where the time goes in v4:
time: 344 us; the launch traced here: 343 us
  waiting for transfers between devices  218 us (63%)
  Pallas kernels  55.1 us (16%)
  starting transfers between devices  29.7 us (9%)
  local copies, waits for them, and re-layouts  16.5 us (5%)
  between operations  13.4 us (4%)
  matrix products  6.24 us (2%)
  other arithmetic  4.47 us (1%)
    ppermute x3, waiting for transfers between devices, send(): return lax.ppermute(value, 'col', step(z, x, core, lax.axis_size('col')))  162 us
    pallas_call x2, Pallas kernels, pair_sums(): pl.pallas_call(functools.partial(sums_kernel, shapes(late), shapes(early)...  28.2 us
    all_to_all x2, waiting for transfers between devices, sum_rows(): lax.all_to_all(slices, 'row', split_axis=0, concat_axis=0, tiled=True)  26.9 us
    pallas_call x2, Pallas kernels, pair_update(): pl.pallas_call(functools.partial(update_kernel, shapes(late), shapes(earl...  26.9 us
    all_to_all x2, waiting for transfers between devices, sum_rows(): lax.all_to_all(copies, 'row', split_axis=0, concat_axis=0, tiled=True)  26.4 us
    all_to_all x2, starting transfers between devices, sum_rows(): lax.all_to_all(slices, 'row', split_axis=0, concat_axis=0, tiled=True)  10.8 us
    reshape x1, local copies, waits for them, and re-layouts, local(): band_vectors.reshape(rows // col_size, col_size, -1).transpose(1, 0, 2)  7.69 us
    all_to_all x2, starting transfers between devices, sum_rows(): lax.all_to_all(copies, 'row', split_axis=0, concat_axis=0, tiled=True)  7.28 us
  transfers between devices with their start and end apart: 11, of which 8 were waited for; matrix products, arithmetic and copies ran while one was open for 6% of the time, Pallas kernels for 8%

profile of v4, /device:TPU:1, one launch (start us, length us, event | category | flops | bytes accessed | tf_op | source)
XLA Modules:
  0.0 342.8 jit_solution(2081499843669432300)
XLA Ops:
  6.5 2.2 slice_bitcast_fusion
  8.9 0.1 slice.65
  9.0 2.5 collective-permute-start
  11.5 7.7 %copy.7 = f32[64,16,8,256]{3,2,0,1:T(8,128)} copy(f32[64,16,8,256]{3,2,1,0:T(8,128)} %bitcast.52) | data formatting | bytes 16777216 | tf_op jit(solution)/shard_map/reshape | solution.py:199
  19.2 26.4 %collective-permute-done = f32[3,16,8192]{2,1,0:T(8,128)S(1)} collective-permute-done((f32[3,16,8192]{2,1,0:T(8,128)S(1)}, f32[3,16,8192]{2,1,0:T(8,128)S(1)}, u32[]{:S(2)}, u32[]{:S(2)}) %collective-permute-start) | collective-permute-done | bytes 1572896 | tf_op jit(solution)/shard_map/ppermute | solution.py:156
  45.6 1.2 copy-done.1
  46.8 1.1 pad_maximum_fusion.1
  48.1 1.1 slice-done
  49.1 1.5 pad_maximum_fusion
  50.6 6.8 %all-to-all-start = ((f32[16,512,256]{2,1,0:T(8,128)}), f32[16,512,256]{2,1,0:T(8,128)}, u32[]{:S(2)}, u32[]{:S(2)}) async-start(f32[16,512,256]{2,1,0:T(8,128)} %bitcast.48), calls=%async_computation | async-start | bytes 16777216 | tf_op jit(solution)/shard_map/all_to_all | solution.py:200
  57.4 1.7 constant_dynamic-slice_fusion
  59.2 1.5 collective-permute-start.1
  60.6 134.1 %collective-permute-done.1.refs_2_ = f32[64,8192]{1,0:T(8,128)S(1)} collective-permute-done((f32[64,8192]{1,0:T(8,128)S(1)}, f32[64,8192]{1,0:T(8,128)S(1)}, u32[]{:S(2)}, u32[]{:S(2)}) %collective-permute-start.1) | collective-permute-done | bytes 2097184 | tf_op jit(solution)/shard_map/ppermute | solution.py:156
  194.7 0.8 collective-permute-start.2
  195.5 0.1 stack.20
  195.7 2.4 all-to-all-done
  198.1 1.3 collective-permute-done.2.refs_3_
  199.4 14.1 %shard_map.37 = f32[768,256]{1,0:T(8,128)} custom-call(f32[256,8192]{1,0:T(8,128)} %all-gather.7.cloned.1.call-done.refs_0_, f32[128,8192]{1,0:T(8,128)} %bitcast.50, f32[64,8192]{1,0:T(8,128)} %copy-done.2, f32[64,8192]{1,0:T(8,128)} %collective-permute-done.2.refs_3_, f32[8192,256]{1,0:T(8,128)} %bitcast.13.refs_4_.refs_5_), custom_call_target="tpu_custom_call" | custom-call | flops 9663676416 | bytes 25165824 | tf_op jit(solution)/shard_map/pallas_call | solution.py:84
  213.5 7.2 %all-to-all-start.1 = ((f32[8,96,256]{2,1,0:T(8,128)}), f32[8,96,256]{2,1,0:T(8,128)S(1)}, u32[]{:S(2)}, u32[]{:S(2)}) async-start(f32[8,96,256]{2,1,0:T(8,128)} %bitcast.62), calls=%async_computation.1 | async-start | bytes 1572864 | tf_op jit(solution)/shard_map/all_to_all | solution.py:142
  220.8 0.1 stack.16
  221.2 1.4 fusion.10
  222.5 12.8 %all-to-all-done.1 = f32[8,96,256]{2,1,0:T(8,128)S(1)} async-done(((f32[8,96,256]{2,1,0:T(8,128)}), f32[8,96,256]{2,1,0:T(8,128)S(1)}, u32[]{:S(2)}, u32[]{:S(2)}) %all-to-all-start.1) | async-done | bytes 786464 | tf_op jit(solution)/shard_map/all_to_all | solution.py:142
  235.4 0.9 broadcast_in_dim.4
  236.3 3.5 %all-to-all-start.2 = ((f32[8,96,256]{2,1,0:T(8,128)}), f32[8,96,256]{2,1,0:T(8,128)S(1)}, u32[]{:S(2)}, u32[]{:S(2)}) async-start(f32[8,96,256]{2,1,0:T(8,128)} %broadcast_in_dim.4), calls=%async_computation.2 | async-start | bytes 1572864 | tf_op jit(solution)/shard_map/all_to_all | solution.py:144
  239.9 0.4 fusion.17
  240.3 0.3 fusion.8
  240.6 0.4 fusion.20
  241.0 13.3 %all-to-all-done.2 = f32[8,96,256]{2,1,0:T(8,128)S(1)} async-done(((f32[8,96,256]{2,1,0:T(8,128)}), f32[8,96,256]{2,1,0:T(8,128)S(1)}, u32[]{:S(2)}, u32[]{:S(2)}) %all-to-all-start.2) | async-done | bytes 786464 | tf_op jit(solution)/shard_map/all_to_all | solution.py:144
  254.3 0.4 fusion.4
  254.7 0.4 convolution_subtract_fusion.1
  255.1 0.4 fusion.40
  255.5 0.8 pad_maximum_fusion.2.refs_4_
  256.3 13.5 %shard_map.38.refs_2_.refs_3_ = f32[8192,256]{1,0:T(8,128)} custom-call(f32[256,8192]{1,0:T(8,128)} %all-gather.7.cloned.1.call-done.refs_0_, f32[128,8192]{1,0:T(8,128)} %bitcast.51, f32[64,8192]{1,0:T(8,128)} %copy-done.2, f32[64,8192]{1,0:T(8,128)} %collective-permute-done.2.refs_3_, f32[512,256]{1,0:T(8,128)} %pad_maximum_fusion.2.refs_4_, ...), custom_call_target="tpu_custom_call" | custom-call | flops 6442450944 | bytes 33554432 | tf_op jit(solution)/shard_map/pallas_call | solution.py:122
  269.8 14.1 %shard_map.39 = f32[768,256]{1,0:T(8,128)} custom-call(f32[2,256,8192]{2,1,0:T(8,128)} %all-gather.5.cloned.1.call-done.refs_0_.refs_1_, f32[2,256,8192]{2,1,0:T(8,128)} %all-gather.5.cloned.1.call-done.refs_0_.refs_1_, f32[8192,256]{1,0:T(8,128)} %shard_map.38.refs_2_.refs_3_), custom_call_target="tpu_custom_call" | custom-call | flops 9663676416 | bytes 25165824 | tf_op jit(solution)/shard_map/pallas_call | solution.py:84
  283.8 3.5 %all-to-all-start.3 = ((f32[8,96,256]{2,1,0:T(8,128)}), f32[8,96,256]{2,1,0:T(8,128)S(1)}, u32[]{:S(2)}, u32[]{:S(2)}) async-start(f32[8,96,256]{2,1,0:T(8,128)} %bitcast.56), calls=%async_computation.3 | async-start | bytes 1572864 | tf_op jit(solution)/shard_map/all_to_all | solution.py:142
  287.4 0.3 fusion.12
  287.7 14.1 %all-to-all-done.3 = f32[8,96,256]{2,1,0:T(8,128)S(1)} async-done(((f32[8,96,256]{2,1,0:T(8,128)}), f32[8,96,256]{2,1,0:T(8,128)S(1)}, u32[]{:S(2)}, u32[]{:S(2)}) %all-to-all-start.3) | async-done | bytes 786464 | tf_op jit(solution)/shard_map/all_to_all | solution.py:142
  301.9 0.9 broadcast_in_dim.5
  302.9 3.7 %all-to-all-start.4 = ((f32[8,96,256]{2,1,0:T(8,128)}), f32[8,96,256]{2,1,0:T(8,128)S(1)}, u32[]{:S(2)}, u32[]{:S(2)}) async-start(f32[8,96,256]{2,1,0:T(8,128)} %broadcast_in_dim.5), calls=%async_computation.4 | async-start | bytes 1572864 | tf_op jit(solution)/shard_map/all_to_all | solution.py:144
  306.6 0.3 fusion.6
  306.9 0.4 fusion.21
  307.4 0.4 fusion.19
  307.8 13.1 %all-to-all-done.4 = f32[8,96,256]{2,1,0:T(8,128)S(1)} async-done(((f32[8,96,256]{2,1,0:T(8,128)}), f32[8,96,256]{2,1,0:T(8,128)S(1)}, u32[]{:S(2)}, u32[]{:S(2)}) %all-to-all-start.4) | async-done | bytes 786464 | tf_op jit(solution)/shard_map/all_to_all | solution.py:144
  320.9 0.4 fusion.1
  321.3 0.4 convolution_subtract_fusion
  321.7 0.4 fusion.41
  322.1 0.8 pad_maximum_fusion.3.refs_2_
  322.9 13.4 %shard_map.40 = f32[8192,256]{1,0:T(8,128)} custom-call(f32[2,256,8192]{2,1,0:T(8,128)} %all-gather.5.cloned.1.call-done.refs_0_.refs_1_, f32[2,256,8192]{2,1,0:T(8,128)} %all-gather.5.cloned.1.call-done.refs_0_.refs_1_, f32[512,256]{1,0:T(8,128)} %pad_maximum_fusion.3.refs_2_, f32[8192,256]{1,0:T(8,128)} %shard_map.38.refs_2_.refs_3_), custom_call_target="tpu_custom_call" | custom-call | flops 6442450944 | bytes 33554432 | tf_op jit(solution)/shard_map/pallas_call | solution.py:122
  (32 shorter events, 0.8 us)
Async XLA Ops:
  6.5 2.3 copy-start
  6.5 41.4 %all-gather.9.cloned.1.call-start = ((), (), s32[]{:S(2)}) async-start(), calls=%async_computation.7 | async-start | bytes 4718592 | tf_op jit(solution)/shard_map/all_gather | solution.py:160
  8.8 190.6 %all-gather.7.cloned.1.call-start = ((), (), s32[]{:S(2)}) async-start(), calls=%async_computation.6 | async-start | bytes 9437184 | tf_op jit(solution)/shard_map/all_gather | solution.py:160
  9.0 36.6 %collective-permute-start = (f32[3,16,8192]{2,1,0:T(8,128)S(1)}, f32[3,16,8192]{2,1,0:T(8,128)S(1)}, u32[]{:S(2)}, u32[]{:S(2)}) collective-permute-start(f32[3,16,8192]{2,1,0:T(8,128)S(1)} %slice.65), channel_id=1, source_target_pairs={{0,8},{1,9},{2,10},{3,11},{4,12},{5,13},{6,14},{7,15},{8,0},{9,1},... | collective-permute-start | bytes 4718600 | tf_op jit(solution)/shard_map/ppermute | solution.py:156
  45.6 1.2 copy-start.1
  47.9 1.2 slice-start
  47.9 221.9 %all-gather.5.cloned.1.call-start = ((), (), s32[]{:S(2)}) async-start(), calls=%async_computation.5 | async-start | bytes 18874368 | tf_op jit(solution)/shard_map/all_gather | solution.py:160
  50.6 147.5 %all-to-all-start = ((f32[16,512,256]{2,1,0:T(8,128)}), f32[16,512,256]{2,1,0:T(8,128)}, u32[]{:S(2)}, u32[]{:S(2)}) async-start(f32[16,512,256]{2,1,0:T(8,128)} %bitcast.48), calls=%async_computation | async-start | bytes 16777216 | tf_op jit(solution)/shard_map/all_to_all | solution.py:200
  57.4 138.3 %copy-start.4 = (s32[16]{0:T(128)S(1)}, s32[16]{0:T(128)}, u32[]{:S(2)}) copy-start(s32[16]{0:T(128)} %constant.165.clone.1) | copy-start | bytes 196
  59.2 135.5 %collective-permute-start.1 = (f32[64,8192]{1,0:T(8,128)S(1)}, f32[64,8192]{1,0:T(8,128)S(1)}, u32[]{:S(2)}, u32[]{:S(2)}) collective-permute-start(f32[64,8192]{1,0:T(8,128)S(1)} %bitcast.61), channel_id=1, source_target_pairs={{0,8},{1,9},{2,10},{3,11},{4,12},{5,13},{6,14},{7,15},{8,0},{9,1},... | collective-permute-start | bytes 6291464 | tf_op jit(solution)/shard_map/ppermute | solution.py:156
  194.7 4.7 %copy-start.2 = (f32[64,8192]{1,0:T(8,128)}, f32[64,8192]{1,0:T(8,128)S(1)}, u32[]{:S(2)}) copy-start(f32[64,8192]{1,0:T(8,128)S(1)} %collective-permute-done.1.refs_2_) | copy-start | bytes 6291460
  194.7 4.7 %collective-permute-start.2 = (f32[64,8192]{1,0:T(8,128)S(1)}, f32[64,8192]{1,0:T(8,128)}, u32[]{:S(2)}, u32[]{:S(2)}) collective-permute-start(f32[64,8192]{1,0:T(8,128)S(1)} %collective-permute-done.1.refs_2_), channel_id=1, source_target_pairs={{0,1},{1,0},{2,3},{3,2},{4,5},{5,4},{6,7},{7,6},{8,9},{9,8},{10,11... | collective-permute-start | bytes 6291464 | tf_op jit(solution)/shard_map/ppermute | solution.py:156
  199.4 21.6 %copy-start.5 = (s32[16]{0:T(128)S(1)}, s32[16]{0:T(128)}, u32[]{:S(2)}) copy-start(s32[16]{0:T(128)} %constant.163.clone.1) | copy-start | bytes 196
  213.5 21.8 %all-to-all-start.1 = ((f32[8,96,256]{2,1,0:T(8,128)}), f32[8,96,256]{2,1,0:T(8,128)S(1)}, u32[]{:S(2)}, u32[]{:S(2)}) async-start(f32[8,96,256]{2,1,0:T(8,128)} %bitcast.62), calls=%async_computation.1 | async-start | bytes 1572864 | tf_op jit(solution)/shard_map/all_to_all | solution.py:142
  221.2 19.1 %copy-start.3 = (f32[4,256,256]{2,1,0:T(8,128)S(1)}, f32[4,256,256]{2,1,0:T(8,128)}, u32[]{:S(2)}) copy-start(f32[4,256,256]{2,1,0:T(8,128)} %param.5) | copy-start | bytes 3145732
  236.3 18.0 %all-to-all-start.2 = ((f32[8,96,256]{2,1,0:T(8,128)}), f32[8,96,256]{2,1,0:T(8,128)S(1)}, u32[]{:S(2)}, u32[]{:S(2)}) async-start(f32[8,96,256]{2,1,0:T(8,128)} %broadcast_in_dim.4), calls=%async_computation.2 | async-start | bytes 1572864 | tf_op jit(solution)/shard_map/all_to_all | solution.py:144
  283.8 18.0 %all-to-all-start.3 = ((f32[8,96,256]{2,1,0:T(8,128)}), f32[8,96,256]{2,1,0:T(8,128)S(1)}, u32[]{:S(2)}, u32[]{:S(2)}) async-start(f32[8,96,256]{2,1,0:T(8,128)} %bitcast.56), calls=%async_computation.3 | async-start | bytes 1572864 | tf_op jit(solution)/shard_map/all_to_all | solution.py:142
  302.9 18.0 %all-to-all-start.4 = ((f32[8,96,256]{2,1,0:T(8,128)}), f32[8,96,256]{2,1,0:T(8,128)S(1)}, u32[]{:S(2)}, u32[]{:S(2)}) async-start(f32[8,96,256]{2,1,0:T(8,128)} %broadcast_in_dim.5), calls=%async_computation.4 | async-start | bytes 1572864 | tf_op jit(solution)/shard_map/all_to_all | solution.py:144
Sparse Core Ops, SparseCore 0:
  9.1 35.6 all-gather.8
  48.0 116.8 all-gather.6
  166.6 89.2 all-gather.4

commit v5 on v4

--- a/solution.py
+++ b/solution.py
@@ -10,7 +10,7 @@
 HIGHEST = lax.Precision.HIGHEST
 TILE = 1024
 DEPTH = 4
-VMEM = 56 * 2**20
+VMEM = 50 * 2**20
 
 X_SIZE = 4
 

time: 344 us -> 340 us (0.988)
  no operation moved by 1% of the time
where the time goes in v5:
time: 340 us; the launch traced here: 339 us
  waiting for transfers between devices  217 us (64%)
  Pallas kernels  52.9 us (16%)
  starting transfers between devices  29.6 us (9%)
  local copies, waits for them, and re-layouts  16.5 us (5%)
  between operations  13.4 us (4%)
  matrix products  7.1 us (2%)
    ppermute x3, waiting for transfers between devices, send(): return lax.ppermute(value, 'col', step(z, x, core, lax.axis_size('col')))  162 us
    pallas_call x2, Pallas kernels, pair_sums(): pl.pallas_call(functools.partial(sums_kernel, shapes(late), shapes(early)...  28.3 us
    all_to_all x2, waiting for transfers between devices, sum_rows(): lax.all_to_all(slices, 'row', split_axis=0, concat_axis=0, tiled=True)  27 us
    all_to_all x2, waiting for transfers between devices, sum_rows(): lax.all_to_all(copies, 'row', split_axis=0, concat_axis=0, tiled=True)  25.5 us
    pallas_call x2, Pallas kernels, pair_update(): pl.pallas_call(functools.partial(update_kernel, shapes(late), shapes(earl...  24.6 us
    all_to_all x2, starting transfers between devices, sum_rows(): lax.all_to_all(slices, 'row', split_axis=0, concat_axis=0, tiled=True)  10.7 us
    reshape x1, local copies, waits for them, and re-layouts, local(): band_vectors.reshape(rows // col_size, col_size, -1).transpose(1, 0, 2)  7.69 us
    all_to_all x2, starting transfers between devices, sum_rows(): lax.all_to_all(copies, 'row', split_axis=0, concat_axis=0, tiled=True)  7.28 us
  transfers between devices with their start and end apart: 11, of which 8 were waited for; matrix products, arithmetic and copies ran while one was open for 6% of the time, Pallas kernels for 8%

profile of v5, /device:TPU:1, one launch (start us, length us, event | category | flops | bytes accessed | tf_op | source)
XLA Modules:
  0.0 339.0 jit_solution(2897280602371177611)
XLA Ops:
  6.5 2.2 slice_bitcast_fusion
  8.8 0.1 slice.65
  9.0 2.5 collective-permute-start
  11.5 7.7 %copy.7 = f32[64,16,8,256]{3,2,0,1:T(8,128)} copy(f32[64,16,8,256]{3,2,1,0:T(8,128)} %bitcast.52) | data formatting | bytes 16777216 | tf_op jit(solution)/shard_map/reshape | solution.py:199
  19.2 26.4 %collective-permute-done = f32[3,16,8192]{2,1,0:T(8,128)S(1)} collective-permute-done((f32[3,16,8192]{2,1,0:T(8,128)S(1)}, f32[3,16,8192]{2,1,0:T(8,128)S(1)}, u32[]{:S(2)}, u32[]{:S(2)}) %collective-permute-start) | collective-permute-done | bytes 1572896 | tf_op jit(solution)/shard_map/ppermute | solution.py:156
  45.6 1.2 copy-done.1
  46.8 1.1 pad_maximum_fusion.1
  48.0 1.1 slice-done
  49.1 1.5 pad_maximum_fusion
  50.6 6.8 %all-to-all-start = ((f32[16,512,256]{2,1,0:T(8,128)}), f32[16,512,256]{2,1,0:T(8,128)}, u32[]{:S(2)}, u32[]{:S(2)}) async-start(f32[16,512,256]{2,1,0:T(8,128)} %bitcast.48), calls=%async_computation | async-start | bytes 16777216 | tf_op jit(solution)/shard_map/all_to_all | solution.py:200
  57.4 1.7 constant_dynamic-slice_fusion
  59.1 1.5 collective-permute-start.1
  60.6 134.1 %collective-permute-done.1.refs_2_ = f32[64,8192]{1,0:T(8,128)S(1)} collective-permute-done((f32[64,8192]{1,0:T(8,128)S(1)}, f32[64,8192]{1,0:T(8,128)S(1)}, u32[]{:S(2)}, u32[]{:S(2)}) %collective-permute-start.1) | collective-permute-done | bytes 2097184 | tf_op jit(solution)/shard_map/ppermute | solution.py:156
  194.6 0.8 collective-permute-start.2
  195.4 0.1 stack.17
  195.5 0.1 stack.20
  195.6 2.4 all-to-all-done
  198.1 1.3 collective-permute-done.2.refs_3_
  199.3 14.1 %shard_map.37 = f32[768,256]{1,0:T(8,128)} custom-call(f32[256,8192]{1,0:T(8,128)} %all-gather.7.cloned.1.call-done.refs_0_, f32[128,8192]{1,0:T(8,128)} %bitcast.50, f32[64,8192]{1,0:T(8,128)S(1)} %collective-permute-done.1.refs_2_, f32[64,8192]{1,0:T(8,128)} %collective-permute-done.2.refs_3_, f32[8192,256]{1,0:T(8,128)} %bitcast.13.refs_4_.refs_5_), custom_call_target="tpu_custom_call" | custom-call | flops 9663676416 | bytes 25165824 | tf_op jit(solution)/shard_map/pallas_call | solution.py:84
  213.5 7.2 %all-to-all-start.1 = ((f32[8,96,256]{2,1,0:T(8,128)}), f32[8,96,256]{2,1,0:T(8,128)S(1)}, u32[]{:S(2)}, u32[]{:S(2)}) async-start(f32[8,96,256]{2,1,0:T(8,128)} %bitcast.14), calls=%async_computation.1 | async-start | bytes 1572864 | tf_op jit(solution)/shard_map/all_to_all | solution.py:142
  220.7 0.1 stack.16
  221.0 0.1 add.174
  221.1 1.3 fusion.10
  222.4 12.8 %all-to-all-done.1 = f32[8,96,256]{2,1,0:T(8,128)S(1)} async-done(((f32[8,96,256]{2,1,0:T(8,128)}), f32[8,96,256]{2,1,0:T(8,128)S(1)}, u32[]{:S(2)}, u32[]{:S(2)}) %all-to-all-start.1) | async-done | bytes 786464 | tf_op jit(solution)/shard_map/all_to_all | solution.py:142
  235.3 0.9 broadcast_in_dim.4
  236.2 3.5 %all-to-all-start.2 = ((f32[8,96,256]{2,1,0:T(8,128)}), f32[8,96,256]{2,1,0:T(8,128)S(1)}, u32[]{:S(2)}, u32[]{:S(2)}) async-start(f32[8,96,256]{2,1,0:T(8,128)} %broadcast_in_dim.4), calls=%async_computation.2 | async-start | bytes 1572864 | tf_op jit(solution)/shard_map/all_to_all | solution.py:144
  239.8 0.4 fusion.17
  240.2 1.3 fusion.8
  241.5 0.4 fusion.20
  241.9 12.4 %all-to-all-done.2 = f32[8,96,256]{2,1,0:T(8,128)S(1)} async-done(((f32[8,96,256]{2,1,0:T(8,128)}), f32[8,96,256]{2,1,0:T(8,128)S(1)}, u32[]{:S(2)}, u32[]{:S(2)}) %all-to-all-start.2) | async-done | bytes 786464 | tf_op jit(solution)/shard_map/all_to_all | solution.py:144
  254.2 0.4 fusion.4
  254.6 0.4 convolution_subtract_fusion.1
  255.0 0.4 fusion.40
  255.4 12.2 %shard_map.38.refs_2_.refs_3_ = f32[8192,256]{1,0:T(8,128)} custom-call(f32[256,8192]{1,0:T(8,128)} %all-gather.7.cloned.1.call-done.refs_0_, f32[128,8192]{1,0:T(8,128)} %bitcast.51, f32[64,8192]{1,0:T(8,128)S(1)} %collective-permute-done.1.refs_2_, f32[64,8192]{1,0:T(8,128)} %collective-permute-done.2.refs_3_, f32[512,256]{1,0:T(8,128)S(1)} %pad_maximum_fusion.2.refs_4_, ...), custom_call_target="tpu_custom_call" | custom-call | flops 6442450944 | bytes 33554432 | tf_op jit(solution)/shard_map/pallas_call | solution.py:122
  267.7 14.1 %shard_map.39 = f32[768,256]{1,0:T(8,128)} custom-call(f32[2,256,8192]{2,1,0:T(8,128)} %all-gather.5.cloned.1.call-done.refs_0_.refs_1_, f32[2,256,8192]{2,1,0:T(8,128)} %all-gather.5.cloned.1.call-done.refs_0_.refs_1_, f32[8192,256]{1,0:T(8,128)} %shard_map.38.refs_2_.refs_3_), custom_call_target="tpu_custom_call" | custom-call | flops 9663676416 | bytes 25165824 | tf_op jit(solution)/shard_map/pallas_call | solution.py:84
  281.8 3.5 %all-to-all-start.3 = ((f32[8,96,256]{2,1,0:T(8,128)}), f32[8,96,256]{2,1,0:T(8,128)S(1)}, u32[]{:S(2)}, u32[]{:S(2)}) async-start(f32[8,96,256]{2,1,0:T(8,128)} %bitcast.17), calls=%async_computation.3 | async-start | bytes 1572864 | tf_op jit(solution)/shard_map/all_to_all | solution.py:142
  285.4 0.3 fusion.12
  285.7 14.1 %all-to-all-done.3 = f32[8,96,256]{2,1,0:T(8,128)S(1)} async-done(((f32[8,96,256]{2,1,0:T(8,128)}), f32[8,96,256]{2,1,0:T(8,128)S(1)}, u32[]{:S(2)}, u32[]{:S(2)}) %all-to-all-start.3) | async-done | bytes 786464 | tf_op jit(solution)/shard_map/all_to_all | solution.py:142
  299.9 0.9 broadcast_in_dim.5
  300.8 3.7 %all-to-all-start.4 = ((f32[8,96,256]{2,1,0:T(8,128)}), f32[8,96,256]{2,1,0:T(8,128)S(1)}, u32[]{:S(2)}, u32[]{:S(2)}) async-start(f32[8,96,256]{2,1,0:T(8,128)} %broadcast_in_dim.5), calls=%async_computation.4 | async-start | bytes 1572864 | tf_op jit(solution)/shard_map/all_to_all | solution.py:144
  304.5 0.3 fusion.6
  304.9 0.4 fusion.21
  305.3 0.4 fusion.19
  305.7 13.1 %all-to-all-done.4 = f32[8,96,256]{2,1,0:T(8,128)S(1)} async-done(((f32[8,96,256]{2,1,0:T(8,128)}), f32[8,96,256]{2,1,0:T(8,128)S(1)}, u32[]{:S(2)}, u32[]{:S(2)}) %all-to-all-start.4) | async-done | bytes 786464 | tf_op jit(solution)/shard_map/all_to_all | solution.py:144
  318.8 0.4 fusion.1
  319.2 0.4 convolution_subtract_fusion
  319.6 0.4 fusion.41
  320.0 12.4 %shard_map.40 = f32[8192,256]{1,0:T(8,128)} custom-call(f32[2,256,8192]{2,1,0:T(8,128)} %all-gather.5.cloned.1.call-done.refs_0_.refs_1_, f32[2,256,8192]{2,1,0:T(8,128)} %all-gather.5.cloned.1.call-done.refs_0_.refs_1_, f32[512,256]{1,0:T(8,128)S(1)} %pad_maximum_fusion.3.refs_2_, f32[8192,256]{1,0:T(8,128)} %shard_map.38.refs_2_.refs_3_), custom_call_target="tpu_custom_call" | custom-call | flops 6442450944 | bytes 33554432 | tf_op jit(solution)/shard_map/pallas_call | solution.py:122
  (30 shorter events, 0.7 us)
Async XLA Ops:
  6.5 2.3 copy-start
  6.5 41.3 %all-gather.9.cloned.1.call-start = ((), (), s32[]{:S(2)}) async-start(), calls=%async_computation.7 | async-start | bytes 4718592 | tf_op jit(solution)/shard_map/all_gather | solution.py:160
  8.8 190.5 %all-gather.7.cloned.1.call-start = ((), (), s32[]{:S(2)}) async-start(), calls=%async_computation.6 | async-start | bytes 9437184 | tf_op jit(solution)/shard_map/all_gather | solution.py:160
  9.0 36.6 %collective-permute-start = (f32[3,16,8192]{2,1,0:T(8,128)S(1)}, f32[3,16,8192]{2,1,0:T(8,128)S(1)}, u32[]{:S(2)}, u32[]{:S(2)}) collective-permute-start(f32[3,16,8192]{2,1,0:T(8,128)S(1)} %slice.65), channel_id=1, source_target_pairs={{0,8},{1,9},{2,10},{3,11},{4,12},{5,13},{6,14},{7,15},{8,0},{9,1},... | collective-permute-start | bytes 4718600 | tf_op jit(solution)/shard_map/ppermute | solution.py:156
  45.6 1.2 copy-start.1
  47.9 1.2 slice-start
  47.9 219.8 %all-gather.5.cloned.1.call-start = ((), (), s32[]{:S(2)}) async-start(), calls=%async_computation.5 | async-start | bytes 18874368 | tf_op jit(solution)/shard_map/all_gather | solution.py:160
  50.6 147.5 %all-to-all-start = ((f32[16,512,256]{2,1,0:T(8,128)}), f32[16,512,256]{2,1,0:T(8,128)}, u32[]{:S(2)}, u32[]{:S(2)}) async-start(f32[16,512,256]{2,1,0:T(8,128)} %bitcast.48), calls=%async_computation | async-start | bytes 16777216 | tf_op jit(solution)/shard_map/all_to_all | solution.py:200
  57.4 138.2 %copy-start.3 = (s32[16]{0:T(128)S(1)}, s32[16]{0:T(128)}, u32[]{:S(2)}) copy-start(s32[16]{0:T(128)} %constant.165.clone.1) | copy-start | bytes 196
  59.1 135.5 %collective-permute-start.1 = (f32[64,8192]{1,0:T(8,128)S(1)}, f32[64,8192]{1,0:T(8,128)S(1)}, u32[]{:S(2)}, u32[]{:S(2)}) collective-permute-start(f32[64,8192]{1,0:T(8,128)S(1)} %bitcast.60), channel_id=1, source_target_pairs={{0,8},{1,9},{2,10},{3,11},{4,12},{5,13},{6,14},{7,15},{8,0},{9,1},... | collective-permute-start | bytes 6291464 | tf_op jit(solution)/shard_map/ppermute | solution.py:156
  194.6 4.7 %collective-permute-start.2 = (f32[64,8192]{1,0:T(8,128)S(1)}, f32[64,8192]{1,0:T(8,128)}, u32[]{:S(2)}, u32[]{:S(2)}) collective-permute-start(f32[64,8192]{1,0:T(8,128)S(1)} %collective-permute-done.1.refs_2_), channel_id=1, source_target_pairs={{0,1},{1,0},{2,3},{3,2},{4,5},{5,4},{6,7},{7,6},{8,9},{9,8},{10,11... | collective-permute-start | bytes 6291464 | tf_op jit(solution)/shard_map/ppermute | solution.py:156
  199.3 21.6 %copy-start.4 = (s32[16]{0:T(128)S(1)}, s32[16]{0:T(128)}, u32[]{:S(2)}) copy-start(s32[16]{0:T(128)} %constant.163.clone.1) | copy-start | bytes 196
  213.5 21.7 %all-to-all-start.1 = ((f32[8,96,256]{2,1,0:T(8,128)}), f32[8,96,256]{2,1,0:T(8,128)S(1)}, u32[]{:S(2)}, u32[]{:S(2)}) async-start(f32[8,96,256]{2,1,0:T(8,128)} %bitcast.14), calls=%async_computation.1 | async-start | bytes 1572864 | tf_op jit(solution)/shard_map/all_to_all | solution.py:142
  236.2 18.0 %all-to-all-start.2 = ((f32[8,96,256]{2,1,0:T(8,128)}), f32[8,96,256]{2,1,0:T(8,128)S(1)}, u32[]{:S(2)}, u32[]{:S(2)}) async-start(f32[8,96,256]{2,1,0:T(8,128)} %broadcast_in_dim.4), calls=%async_computation.2 | async-start | bytes 1572864 | tf_op jit(solution)/shard_map/all_to_all | solution.py:144
  267.7 17.7 %copy-start.2 = (f32[4,256,256]{2,1,0:T(8,128)S(1)}, f32[4,256,256]{2,1,0:T(8,128)}, u32[]{:S(2)}) copy-start(f32[4,256,256]{2,1,0:T(8,128)} %param.5) | copy-start | bytes 3145732
  281.8 18.0 %all-to-all-start.3 = ((f32[8,96,256]{2,1,0:T(8,128)}), f32[8,96,256]{2,1,0:T(8,128)S(1)}, u32[]{:S(2)}, u32[]{:S(2)}) async-start(f32[8,96,256]{2,1,0:T(8,128)} %bitcast.17), calls=%async_computation.3 | async-start | bytes 1572864 | tf_op jit(solution)/shard_map/all_to_all | solution.py:142
  300.8 18.0 %all-to-all-start.4 = ((f32[8,96,256]{2,1,0:T(8,128)}), f32[8,96,256]{2,1,0:T(8,128)S(1)}, u32[]{:S(2)}, u32[]{:S(2)}) async-start(f32[8,96,256]{2,1,0:T(8,128)} %broadcast_in_dim.5), calls=%async_computation.4 | async-start | bytes 1572864 | tf_op jit(solution)/shard_map/all_to_all | solution.py:144
Sparse Core Ops, SparseCore 0:
  9.1 35.6 all-gather.8
  48.0 116.8 all-gather.6
  166.6 89.2 all-gather.4

commit v6 on v5

--- a/solution.py
+++ b/solution.py
@@ -97,14 +97,24 @@
 
 def update_kernel(late, early, *refs):
     n_late, n_early = len(late), len(early)
+    count = n_late + n_early
     panels = views(refs, late + early)
-    coeffs_ref, vectors_ref, out_ref = refs[n_late + n_early :]
+    sums_ref, late_t_ref, early_t_ref, vectors_ref, out_ref, high_ref, low_ref = refs[count:]
     rows, columns = vectors_ref.shape
-    coeffs = split(coeffs_ref[...])
+    size = late_t_ref.shape[0]
 
     def body(*tiles):
-        both = split(read((*tiles[n_late : n_late + n_early], *tiles[:n_late])))
-        tiles[-1][...] = tiles[-2][...] - three_pass(both, coeffs, ((0,), (0,)))
+        @pl.when(pl.program_id(0) == 0)
+        def _():
+            early_coeffs = exact(early_t_ref[...], sums_ref[0:size, :])
+            rest = sums_ref[size : 2 * size, :] - exact(sums_ref[2 * size : 3 * size, :], early_coeffs)
+            high, low = split(jnp.concatenate([early_coeffs, exact(late_t_ref[...], rest)], 0))
+            high_ref[...] = high
+            low_ref[...] = low
+
+        both = split(read((*tiles[n_late:count], *tiles[:n_late])))
+        change = three_pass(both, (high_ref[...], low_ref[...]), ((0,), (0,)))
+        tiles[-1][...] = tiles[-2][...] - change
 
     block = buffered((TILE, columns), lambda i: (i, 0))
     pltpu.emit_pipeline(
@@ -115,26 +125,24 @@
     )(*panels, vectors_ref, out_ref)
 
 
-def pair_update(late, early, coeffs, vectors):
+def pair_update(late, early, sums, late_t, early_t, vectors):
     rows, columns = vectors.shape
     size = height(late)
     anywhere = pl.BlockSpec(memory_space=pl.ANY)
+    vmem = pl.BlockSpec(memory_space=pltpu.VMEM)
     return pl.pallas_call(
         functools.partial(update_kernel, shapes(late), shapes(early)),
-        in_specs=[
-            *[anywhere] * (len(late) + len(early)),
-            pl.BlockSpec(memory_space=pltpu.VMEM),
-            anywhere,
-        ],
+        in_specs=[*[anywhere] * (len(late) + len(early)), vmem, vmem, vmem, anywhere],
         out_specs=anywhere,
         out_shape=jax.ShapeDtypeStruct((rows, columns), jnp.float32),
+        scratch_shapes=[pltpu.VMEM((2 * size, columns), jnp.bfloat16)] * 2,
         compiler_params=pltpu.CompilerParams(vmem_limit_bytes=VMEM),
         cost_estimate=pl.CostEstimate(
             flops=12 * size * rows * columns,
             bytes_accessed=4 * rows * (2 * size + 2 * columns),
             transcendentals=0,
         ),
-    )(*arrays(late + early), coeffs, vectors)
+    )(*arrays(late + early), sums, late_t, early_t, vectors)
 
 
 def sum_rows(values, size):
@@ -177,12 +185,8 @@
 
 
 def apply_pair(late, early, late_t, early_t, vectors, row_size):
-    size = late_t.shape[0]
     sums = sum_rows(pair_sums(late, early, vectors), row_size)
-    early_coeffs = exact(early_t, sums[:size])
-    rest = sums[size : 2 * size] - exact(sums[2 * size :], early_coeffs)
-    coeffs = jnp.concatenate([early_coeffs, exact(late_t, rest)], 0)
-    return pair_update(late, early, coeffs, vectors)
+    return pair_update(late, early, sums, late_t, early_t, vectors)
 
 
 def solution(mesh):

time: 340 us -> 339 us (level)
    dot_general x14 -> x8, matrix products: 7.1 us -> 4.82 us  [exact(): jnp.matmul(a, b, precision=HIGHEST, preferred_element_type=jnp.float32)]
  transfers between devices with their start and end apart: 11 -> 11, of which waited for: 8 -> 8; matrix products, arithmetic and copies ran while one was open for 6% -> 5% of each run, Pallas kernels for 8% -> 8%
where the time goes in v6:
time: 339 us; the launch traced here: 338 us
  waiting for transfers between devices  217 us (64%)
  Pallas kernels  54.6 us (16%)
  starting transfers between devices  29.6 us (9%)
  local copies, waits for them, and re-layouts  16.5 us (5%)
  between operations  13.3 us (4%)
  matrix products  4.82 us (1%)
    ppermute x3, waiting for transfers between devices, send(): return lax.ppermute(value, 'col', step(z, x, core, lax.axis_size('col')))  162 us
    pallas_call x2, Pallas kernels, pair_sums(): pl.pallas_call(functools.partial(sums_kernel, shapes(late), shapes(early)...  28.3 us
    all_to_all x2, waiting for transfers between devices, sum_rows(): lax.all_to_all(slices, 'row', split_axis=0, concat_axis=0, tiled=True)  27 us
    pallas_call x2, Pallas kernels, pair_update(): pl.pallas_call(functools.partial(update_kernel, shapes(late), shapes(earl...  26.3 us
    all_to_all x2, waiting for transfers between devices, sum_rows(): lax.all_to_all(copies, 'row', split_axis=0, concat_axis=0, tiled=True)  25.5 us
    all_to_all x2, starting transfers between devices, sum_rows(): lax.all_to_all(slices, 'row', split_axis=0, concat_axis=0, tiled=True)  10.7 us
    reshape x1, local copies, waits for them, and re-layouts, local(): band_vectors.reshape(rows // col_size, col_size, -1).transpose(1, 0, 2)  7.69 us
    all_to_all x2, starting transfers between devices, sum_rows(): lax.all_to_all(copies, 'row', split_axis=0, concat_axis=0, tiled=True)  7.28 us
  transfers between devices with their start and end apart: 11, of which 8 were waited for; matrix products, arithmetic and copies ran while one was open for 5% of the time, Pallas kernels for 8%

profile of v6, /device:TPU:1, one launch (start us, length us, event | category | flops | bytes accessed | tf_op | source)
XLA Modules:
  0.0 338.3 jit_solution(2348160330324954730)
XLA Ops:
  6.5 2.2 slice_bitcast_fusion
  8.8 0.1 slice.41
  9.0 2.5 collective-permute-start
  11.5 7.7 %copy.7 = f32[64,16,8,256]{3,2,0,1:T(8,128)} copy(f32[64,16,8,256]{3,2,1,0:T(8,128)} %bitcast.46) | data formatting | bytes 16777216 | tf_op jit(solution)/shard_map/reshape | solution.py:203
  19.2 26.4 %collective-permute-done = f32[3,16,8192]{2,1,0:T(8,128)S(1)} collective-permute-done((f32[3,16,8192]{2,1,0:T(8,128)S(1)}, f32[3,16,8192]{2,1,0:T(8,128)S(1)}, u32[]{:S(2)}, u32[]{:S(2)}) %collective-permute-start) | collective-permute-done | bytes 1572896 | tf_op jit(solution)/shard_map/ppermute | solution.py:164
  45.6 1.2 copy-done.1
  46.8 1.1 pad_maximum_fusion.1
  48.0 0.1 slice.40
  48.0 1.1 slice-done
  49.1 1.5 pad_maximum_fusion
  50.6 6.8 %all-to-all-start = ((f32[16,512,256]{2,1,0:T(8,128)}), f32[16,512,256]{2,1,0:T(8,128)}, u32[]{:S(2)}, u32[]{:S(2)}) async-start(f32[16,512,256]{2,1,0:T(8,128)} %bitcast.42), calls=%async_computation | async-start | bytes 16777216 | tf_op jit(solution)/shard_map/all_to_all | solution.py:204
  57.4 1.7 constant_dynamic-slice_fusion
  59.1 1.5 collective-permute-start.1
  60.6 134.1 %collective-permute-done.1.refs_2_ = f32[64,8192]{1,0:T(8,128)S(1)} collective-permute-done((f32[64,8192]{1,0:T(8,128)S(1)}, f32[64,8192]{1,0:T(8,128)S(1)}, u32[]{:S(2)}, u32[]{:S(2)}) %collective-permute-start.1) | collective-permute-done | bytes 2097184 | tf_op jit(solution)/shard_map/ppermute | solution.py:164
  194.6 0.8 collective-permute-start.2
  195.4 0.1 stack.17
  195.5 0.1 stack.20
  195.6 2.4 all-to-all-done
  198.1 1.3 collective-permute-done.2.refs_3_
  199.3 14.1 %shard_map.37 = f32[768,256]{1,0:T(8,128)} custom-call(f32[256,8192]{1,0:T(8,128)} %all-gather.7.cloned.1.call-done.refs_0_, f32[128,8192]{1,0:T(8,128)} %bitcast.44, f32[64,8192]{1,0:T(8,128)S(1)} %collective-permute-done.1.refs_2_, f32[64,8192]{1,0:T(8,128)} %collective-permute-done.2.refs_3_, f32[8192,256]{1,0:T(8,128)} %bitcast.7.refs_4_.refs_7_), custom_call_target="tpu_custom_call" | custom-call | flops 9663676416 | bytes 25165824 | tf_op jit(solution)/shard_map/pallas_call | solution.py:84
  213.5 7.2 %all-to-all-start.1 = ((f32[8,96,256]{2,1,0:T(8,128)}), f32[8,96,256]{2,1,0:T(8,128)S(1)}, u32[]{:S(2)}, u32[]{:S(2)}) async-start(f32[8,96,256]{2,1,0:T(8,128)} %bitcast.8), calls=%async_computation.1 | async-start | bytes 1572864 | tf_op jit(solution)/shard_map/all_to_all | solution.py:150
  220.7 0.1 iota_add_fusion
  220.7 0.1 stack.16
  220.8 0.1 add.185
  220.9 0.1 iota_add_fusion.1
  221.0 0.1 add.176
  221.1 1.3 fusion.4
  222.4 12.8 %all-to-all-done.1 = f32[8,96,256]{2,1,0:T(8,128)S(1)} async-done(((f32[8,96,256]{2,1,0:T(8,128)}), f32[8,96,256]{2,1,0:T(8,128)S(1)}, u32[]{:S(2)}, u32[]{:S(2)}) %all-to-all-start.1) | async-done | bytes 786464 | tf_op jit(solution)/shard_map/all_to_all | solution.py:150
  235.2 0.1 reduce_sum.18
  235.3 0.9 broadcast_in_dim.4
  236.2 3.5 %all-to-all-start.2 = ((f32[8,96,256]{2,1,0:T(8,128)}), f32[8,96,256]{2,1,0:T(8,128)S(1)}, u32[]{:S(2)}, u32[]{:S(2)}) async-start(f32[8,96,256]{2,1,0:T(8,128)} %broadcast_in_dim.4), calls=%async_computation.2 | async-start | bytes 1572864 | tf_op jit(solution)/shard_map/all_to_all | solution.py:152
  239.8 0.4 fusion.11.refs_6_
  240.2 1.3 fusion.6
  241.5 0.4 fusion.15.refs_5_
  241.9 12.4 %all-to-all-done.2 = f32[8,96,256]{2,1,0:T(8,128)S(1)} async-done(((f32[8,96,256]{2,1,0:T(8,128)}), f32[8,96,256]{2,1,0:T(8,128)S(1)}, u32[]{:S(2)}, u32[]{:S(2)}) %all-to-all-start.2) | async-done | bytes 786464 | tf_op jit(solution)/shard_map/all_to_all | solution.py:152
  254.2 12.9 %shard_map.38.refs_2_.refs_5_ = f32[8192,256]{1,0:T(8,128)} custom-call(f32[256,8192]{1,0:T(8,128)} %all-gather.7.cloned.1.call-done.refs_0_, f32[128,8192]{1,0:T(8,128)} %bitcast.45, f32[64,8192]{1,0:T(8,128)S(1)} %collective-permute-done.1.refs_2_, f32[64,8192]{1,0:T(8,128)} %collective-permute-done.2.refs_3_, f32[768,256]{1,0:T(8,128)S(1)} %bitcast.40, ...), custom_call_target="tpu_custom_call" | custom-call | flops 6442450944 | bytes 33554432 | tf_op jit(solution)/shard_map/pallas_call | solution.py:133
  267.2 14.1 %shard_map.39 = f32[768,256]{1,0:T(8,128)} custom-call(f32[2,256,8192]{2,1,0:T(8,128)} %all-gather.5.cloned.1.call-done.refs_0_.refs_1_, f32[2,256,8192]{2,1,0:T(8,128)} %all-gather.5.cloned.1.call-done.refs_0_.refs_1_, f32[8192,256]{1,0:T(8,128)} %shard_map.38.refs_2_.refs_5_), custom_call_target="tpu_custom_call" | custom-call | flops 9663676416 | bytes 25165824 | tf_op jit(solution)/shard_map/pallas_call | solution.py:84
  281.3 3.5 %all-to-all-start.3 = ((f32[8,96,256]{2,1,0:T(8,128)}), f32[8,96,256]{2,1,0:T(8,128)S(1)}, u32[]{:S(2)}, u32[]{:S(2)}) async-start(f32[8,96,256]{2,1,0:T(8,128)} %bitcast.16), calls=%async_computation.3 | async-start | bytes 1572864 | tf_op jit(solution)/shard_map/all_to_all | solution.py:150
  284.9 0.3 fusion
  285.2 14.1 %all-to-all-done.3 = f32[8,96,256]{2,1,0:T(8,128)S(1)} async-done(((f32[8,96,256]{2,1,0:T(8,128)}), f32[8,96,256]{2,1,0:T(8,128)S(1)}, u32[]{:S(2)}, u32[]{:S(2)}) %all-to-all-start.3) | async-done | bytes 786464 | tf_op jit(solution)/shard_map/all_to_all | solution.py:150
  299.3 0.1 reduce_sum.19
  299.4 0.9 broadcast_in_dim.5
  300.3 3.7 %all-to-all-start.4 = ((f32[8,96,256]{2,1,0:T(8,128)}), f32[8,96,256]{2,1,0:T(8,128)S(1)}, u32[]{:S(2)}, u32[]{:S(2)}) async-start(f32[8,96,256]{2,1,0:T(8,128)} %broadcast_in_dim.5), calls=%async_computation.4 | async-start | bytes 1572864 | tf_op jit(solution)/shard_map/all_to_all | solution.py:152
  304.0 0.3 fusion.2
  304.4 0.4 fusion.13.refs_4_
  304.8 0.4 fusion.14.refs_3_
  305.2 13.1 %all-to-all-done.4 = f32[8,96,256]{2,1,0:T(8,128)S(1)} async-done(((f32[8,96,256]{2,1,0:T(8,128)}), f32[8,96,256]{2,1,0:T(8,128)S(1)}, u32[]{:S(2)}, u32[]{:S(2)}) %all-to-all-start.4) | async-done | bytes 786464 | tf_op jit(solution)/shard_map/all_to_all | solution.py:152
  318.3 13.4 %shard_map.40 = f32[8192,256]{1,0:T(8,128)} custom-call(f32[2,256,8192]{2,1,0:T(8,128)} %all-gather.5.cloned.1.call-done.refs_0_.refs_1_, f32[2,256,8192]{2,1,0:T(8,128)} %all-gather.5.cloned.1.call-done.refs_0_.refs_1_, f32[768,256]{1,0:T(8,128)S(1)} %bitcast.41, f32[256,256]{1,0:T(8,128)S(1)} %fusion.14.refs_3_, f32[256,256]{1,0:T(8,128)S(1)} %fusion.13.refs_4_, ...), custom_call_target="tpu_custom_call" | custom-call | flops 6442450944 | bytes 33554432 | tf_op jit(solution)/shard_map/pallas_call | solution.py:133
  (22 shorter events, 0.2 us)
Async XLA Ops:
  6.5 2.3 copy-start
  6.5 41.3 %all-gather.9.cloned.1.call-start = ((), (), s32[]{:S(2)}) async-start(), calls=%async_computation.7 | async-start | bytes 4718592 | tf_op jit(solution)/shard_map/all_gather | solution.py:168
  8.8 190.5 %all-gather.7.cloned.1.call-start = ((), (), s32[]{:S(2)}) async-start(), calls=%async_computation.6 | async-start | bytes 9437184 | tf_op jit(solution)/shard_map/all_gather | solution.py:168
  9.0 36.6 %collective-permute-start = (f32[3,16,8192]{2,1,0:T(8,128)S(1)}, f32[3,16,8192]{2,1,0:T(8,128)S(1)}, u32[]{:S(2)}, u32[]{:S(2)}) collective-permute-start(f32[3,16,8192]{2,1,0:T(8,128)S(1)} %slice.41), channel_id=1, source_target_pairs={{0,8},{1,9},{2,10},{3,11},{4,12},{5,13},{6,14},{7,15},{8,0},{9,1},... | collective-permute-start | bytes 4718600 | tf_op jit(solution)/shard_map/ppermute | solution.py:164
  45.6 1.2 copy-start.1
  47.9 1.2 slice-start
  47.9 219.3 %all-gather.5.cloned.1.call-start = ((), (), s32[]{:S(2)}) async-start(), calls=%async_computation.5 | async-start | bytes 18874368 | tf_op jit(solution)/shard_map/all_gather | solution.py:168
  50.6 147.5 %all-to-all-start = ((f32[16,512,256]{2,1,0:T(8,128)}), f32[16,512,256]{2,1,0:T(8,128)}, u32[]{:S(2)}, u32[]{:S(2)}) async-start(f32[16,512,256]{2,1,0:T(8,128)} %bitcast.42), calls=%async_computation | async-start | bytes 16777216 | tf_op jit(solution)/shard_map/all_to_all | solution.py:204
  57.4 138.2 %copy-start.3 = (s32[16]{0:T(128)S(1)}, s32[16]{0:T(128)}, u32[]{:S(2)}) copy-start(s32[16]{0:T(128)} %constant.166.clone.1) | copy-start | bytes 196
  59.1 135.5 %collective-permute-start.1 = (f32[64,8192]{1,0:T(8,128)S(1)}, f32[64,8192]{1,0:T(8,128)S(1)}, u32[]{:S(2)}, u32[]{:S(2)}) collective-permute-start(f32[64,8192]{1,0:T(8,128)S(1)} %bitcast.50), channel_id=1, source_target_pairs={{0,8},{1,9},{2,10},{3,11},{4,12},{5,13},{6,14},{7,15},{8,0},{9,1},... | collective-permute-start | bytes 6291464 | tf_op jit(solution)/shard_map/ppermute | solution.py:164
  194.6 4.7 %collective-permute-start.2 = (f32[64,8192]{1,0:T(8,128)S(1)}, f32[64,8192]{1,0:T(8,128)}, u32[]{:S(2)}, u32[]{:S(2)}) collective-permute-start(f32[64,8192]{1,0:T(8,128)S(1)} %collective-permute-done.1.refs_2_), channel_id=1, source_target_pairs={{0,1},{1,0},{2,3},{3,2},{4,5},{5,4},{6,7},{7,6},{8,9},{9,8},{10,11... | collective-permute-start | bytes 6291464 | tf_op jit(solution)/shard_map/ppermute | solution.py:164
  199.3 21.6 %copy-start.4 = (s32[16]{0:T(128)S(1)}, s32[16]{0:T(128)}, u32[]{:S(2)}) copy-start(s32[16]{0:T(128)} %constant.164.clone.1) | copy-start | bytes 196
  213.5 21.7 %all-to-all-start.1 = ((f32[8,96,256]{2,1,0:T(8,128)}), f32[8,96,256]{2,1,0:T(8,128)S(1)}, u32[]{:S(2)}, u32[]{:S(2)}) async-start(f32[8,96,256]{2,1,0:T(8,128)} %bitcast.8), calls=%async_computation.1 | async-start | bytes 1572864 | tf_op jit(solution)/shard_map/all_to_all | solution.py:150
  236.2 18.0 %all-to-all-start.2 = ((f32[8,96,256]{2,1,0:T(8,128)}), f32[8,96,256]{2,1,0:T(8,128)S(1)}, u32[]{:S(2)}, u32[]{:S(2)}) async-start(f32[8,96,256]{2,1,0:T(8,128)} %broadcast_in_dim.4), calls=%async_computation.2 | async-start | bytes 1572864 | tf_op jit(solution)/shard_map/all_to_all | solution.py:152
  267.2 17.7 %copy-start.2 = (f32[4,256,256]{2,1,0:T(8,128)S(1)}, f32[4,256,256]{2,1,0:T(8,128)}, u32[]{:S(2)}) copy-start(f32[4,256,256]{2,1,0:T(8,128)} %param.5) | copy-start | bytes 3145732
  281.3 18.0 %all-to-all-start.3 = ((f32[8,96,256]{2,1,0:T(8,128)}), f32[8,96,256]{2,1,0:T(8,128)S(1)}, u32[]{:S(2)}, u32[]{:S(2)}) async-start(f32[8,96,256]{2,1,0:T(8,128)} %bitcast.16), calls=%async_computation.3 | async-start | bytes 1572864 | tf_op jit(solution)/shard_map/all_to_all | solution.py:150
  300.3 18.0 %all-to-all-start.4 = ((f32[8,96,256]{2,1,0:T(8,128)}), f32[8,96,256]{2,1,0:T(8,128)S(1)}, u32[]{:S(2)}, u32[]{:S(2)}) async-start(f32[8,96,256]{2,1,0:T(8,128)} %broadcast_in_dim.5), calls=%async_computation.4 | async-start | bytes 1572864 | tf_op jit(solution)/shard_map/all_to_all | solution.py:152
Sparse Core Ops, SparseCore 0:
  9.1 35.6 all-gather.8
  48.0 116.8 all-gather.6
  166.6 89.2 all-gather.4

commit v7 on v6

--- a/solution.py
+++ b/solution.py
@@ -145,10 +145,14 @@
     )(*arrays(late + early), sums, late_t, early_t, vectors)
 
 
+def add_kernel(slices_ref, copies_ref):
+    copies_ref[...] = jnp.broadcast_to(jnp.sum(slices_ref[...], 0, keepdims=True), copies_ref.shape)
+
+
 def sum_rows(values, size):
     slices = values.reshape(size, values.shape[0] // size, values.shape[1])
-    mine = lax.all_to_all(slices, "row", split_axis=0, concat_axis=0, tiled=True).sum(0)
-    copies = jnp.broadcast_to(mine[None], slices.shape)
+    slices = lax.all_to_all(slices, "row", split_axis=0, concat_axis=0, tiled=True)
+    copies = pl.pallas_call(add_kernel, out_shape=jax.ShapeDtypeStruct(slices.shape, slices.dtype))(slices)
     return lax.all_to_all(copies, "row", split_axis=0, concat_axis=0, tiled=True).reshape(values.shape)
 
 

time: 339 us -> 343 us (1.012)
  Pallas kernels: 54.6 us -> 58.9 us
    pallas_call x0 -> x2, Pallas kernels: none -> 4.24 us  [sum_rows(): pl.pallas_call(add_kernel, out_shape=jax.ShapeDtypeStruct(slices.shape, s...]
  transfers between devices with their start and end apart: 11 -> 11, of which waited for: 8 -> 8; matrix products, arithmetic and copies ran while one was open for 5% -> 5% of each run, Pallas kernels for 8% -> 9%
where the time goes in v7:
time: 343 us; the launch traced here: 342 us
  waiting for transfers between devices  217 us (63%)
  Pallas kernels  58.9 us (17%)
  starting transfers between devices  29.7 us (9%)
  local copies, waits for them, and re-layouts  16.4 us (5%)
  between operations  13.3 us (4%)
  matrix products  4.82 us (1%)
    ppermute x3, waiting for transfers between devices, send(): return lax.ppermute(value, 'col', step(z, x, core, lax.axis_size('col')))  162 us
    pallas_call x2, Pallas kernels, pair_sums(): pl.pallas_call(functools.partial(sums_kernel, shapes(late), shapes(early)...  28.3 us
    all_to_all x2, waiting for transfers between devices, sum_rows(): lax.all_to_all(slices, 'row', split_axis=0, concat_axis=0, tiled=True)  27 us
    pallas_call x2, Pallas kernels, pair_update(): pl.pallas_call(functools.partial(update_kernel, shapes(late), shapes(earl...  26.4 us
    all_to_all x2, waiting for transfers between devices, sum_rows(): lax.all_to_all(copies, 'row', split_axis=0, concat_axis=0, tiled=True)  25.5 us
    all_to_all x2, starting transfers between devices, sum_rows(): lax.all_to_all(slices, 'row', split_axis=0, concat_axis=0, tiled=True)  10.8 us
    reshape x1, local copies, waits for them, and re-layouts, local(): band_vectors.reshape(rows // col_size, col_size, -1).transpose(1, 0, 2)  7.69 us
    all_to_all x2, starting transfers between devices, sum_rows(): lax.all_to_all(copies, 'row', split_axis=0, concat_axis=0, tiled=True)  7.27 us
  transfers between devices with their start and end apart: 11, of which 8 were waited for; matrix products, arithmetic and copies ran while one was open for 5% of the time, Pallas kernels for 9%

profile of v7, /device:TPU:1, one launch (start us, length us, event | category | flops | bytes accessed | tf_op | source)
XLA Modules:
  0.0 342.4 jit_solution(66172908723557094)
XLA Ops:
  6.5 2.2 slice_bitcast_fusion
  8.8 0.1 slice.41
  9.0 2.5 collective-permute-start
  11.5 7.7 %copy.7 = f32[64,16,8,256]{3,2,0,1:T(8,128)} copy(f32[64,16,8,256]{3,2,1,0:T(8,128)} %bitcast.46) | data formatting | bytes 16777216 | tf_op jit(solution)/shard_map/reshape | solution.py:207
  19.2 26.4 %collective-permute-done = f32[3,16,8192]{2,1,0:T(8,128)S(1)} collective-permute-done((f32[3,16,8192]{2,1,0:T(8,128)S(1)}, f32[3,16,8192]{2,1,0:T(8,128)S(1)}, u32[]{:S(2)}, u32[]{:S(2)}) %collective-permute-start) | collective-permute-done | bytes 1572896 | tf_op jit(solution)/shard_map/ppermute | solution.py:168
  45.6 1.2 copy-done.1
  46.8 1.0 pad_maximum_fusion.1
  48.0 0.1 slice.40
  48.0 1.1 slice-done
  49.1 1.5 pad_maximum_fusion
  50.6 6.8 %all-to-all-start = ((f32[16,512,256]{2,1,0:T(8,128)}), f32[16,512,256]{2,1,0:T(8,128)}, u32[]{:S(2)}, u32[]{:S(2)}) async-start(f32[16,512,256]{2,1,0:T(8,128)} %bitcast.42), calls=%async_computation | async-start | bytes 16777216 | tf_op jit(solution)/shard_map/all_to_all | solution.py:208
  57.4 1.7 constant_dynamic-slice_fusion
  59.2 1.5 collective-permute-start.1
  60.6 134.1 %collective-permute-done.1.refs_2_ = f32[64,8192]{1,0:T(8,128)S(1)} collective-permute-done((f32[64,8192]{1,0:T(8,128)S(1)}, f32[64,8192]{1,0:T(8,128)S(1)}, u32[]{:S(2)}, u32[]{:S(2)}) %collective-permute-start.1) | collective-permute-done | bytes 2097184 | tf_op jit(solution)/shard_map/ppermute | solution.py:168
  194.7 0.8 collective-permute-start.2
  195.5 0.1 stack.17
  195.5 0.1 stack.20
  195.7 2.4 all-to-all-done
  198.1 1.3 collective-permute-done.2.refs_3_
  199.4 14.1 %shard_map.37 = f32[768,256]{1,0:T(8,128)} custom-call(f32[256,8192]{1,0:T(8,128)} %all-gather.7.cloned.1.call-done.refs_0_, f32[128,8192]{1,0:T(8,128)} %bitcast.44, f32[64,8192]{1,0:T(8,128)S(1)} %collective-permute-done.1.refs_2_, f32[64,8192]{1,0:T(8,128)} %collective-permute-done.2.refs_3_, f32[8192,256]{1,0:T(8,128)} %bitcast.7.refs_4_.refs_7_), custom_call_target="tpu_custom_call" | custom-call | flops 9663676416 | bytes 25165824 | tf_op jit(solution)/shard_map/pallas_call | solution.py:84
  213.5 7.2 %all-to-all-start.1 = ((f32[8,96,256]{2,1,0:T(8,128)}), f32[8,96,256]{2,1,0:T(8,128)S(1)}, u32[]{:S(2)}, u32[]{:S(2)}) async-start(f32[8,96,256]{2,1,0:T(8,128)} %bitcast.8), calls=%async_computation.1 | async-start | bytes 1572864 | tf_op jit(solution)/shard_map/all_to_all | solution.py:154
  220.7 0.1 iota_add_fusion
  220.8 0.1 stack.16
  220.9 0.1 add.185
  221.0 0.1 iota_add_fusion.1
  221.1 0.1 add.176
  221.2 1.3 fusion.4
  222.4 12.8 %all-to-all-done.1.slices_ref = f32[8,96,256]{2,1,0:T(8,128)S(1)} async-done(((f32[8,96,256]{2,1,0:T(8,128)}), f32[8,96,256]{2,1,0:T(8,128)S(1)}, u32[]{:S(2)}, u32[]{:S(2)}) %all-to-all-start.1) | async-done | bytes 786464 | tf_op jit(solution)/shard_map/all_to_all | solution.py:154
  235.3 0.9 copy-done.2
  236.2 2.1 shard_map.38
  238.3 3.5 %all-to-all-start.2 = ((f32[8,96,256]{2,1,0:T(8,128)}), f32[8,96,256]{2,1,0:T(8,128)S(1)}, u32[]{:S(2)}, u32[]{:S(2)}) async-start(f32[8,96,256]{2,1,0:T(8,128)} %shard_map.38), calls=%async_computation.2 | async-start | bytes 1572864 | tf_op jit(solution)/shard_map/all_to_all | solution.py:156
  241.9 0.4 fusion.11.refs_6_
  242.3 1.3 fusion.6
  243.6 0.4 fusion.15.refs_5_
  244.0 12.4 %all-to-all-done.2 = f32[8,96,256]{2,1,0:T(8,128)S(1)} async-done(((f32[8,96,256]{2,1,0:T(8,128)}), f32[8,96,256]{2,1,0:T(8,128)S(1)}, u32[]{:S(2)}, u32[]{:S(2)}) %all-to-all-start.2) | async-done | bytes 786464 | tf_op jit(solution)/shard_map/all_to_all | solution.py:156
  256.3 12.9 %shard_map.39.refs_2_.refs_5_ = f32[8192,256]{1,0:T(8,128)} custom-call(f32[256,8192]{1,0:T(8,128)} %all-gather.7.cloned.1.call-done.refs_0_, f32[128,8192]{1,0:T(8,128)} %bitcast.45, f32[64,8192]{1,0:T(8,128)S(1)} %collective-permute-done.1.refs_2_, f32[64,8192]{1,0:T(8,128)} %collective-permute-done.2.refs_3_, f32[768,256]{1,0:T(8,128)S(1)} %bitcast.40, ...), custom_call_target="tpu_custom_call" | custom-call | flops 6442450944 | bytes 33554432 | tf_op jit(solution)/shard_map/pallas_call | solution.py:133
  269.3 14.1 %shard_map.40 = f32[768,256]{1,0:T(8,128)} custom-call(f32[2,256,8192]{2,1,0:T(8,128)} %all-gather.5.cloned.1.call-done.refs_0_.refs_1_, f32[2,256,8192]{2,1,0:T(8,128)} %all-gather.5.cloned.1.call-done.refs_0_.refs_1_, f32[8192,256]{1,0:T(8,128)} %shard_map.39.refs_2_.refs_5_), custom_call_target="tpu_custom_call" | custom-call | flops 9663676416 | bytes 25165824 | tf_op jit(solution)/shard_map/pallas_call | solution.py:84
  283.4 3.5 %all-to-all-start.3 = ((f32[8,96,256]{2,1,0:T(8,128)}), f32[8,96,256]{2,1,0:T(8,128)S(1)}, u32[]{:S(2)}, u32[]{:S(2)}) async-start(f32[8,96,256]{2,1,0:T(8,128)} %bitcast.16), calls=%async_computation.3 | async-start | bytes 1572864 | tf_op jit(solution)/shard_map/all_to_all | solution.py:154
  287.0 0.3 fusion
  287.3 14.1 %all-to-all-done.3.slices_ref = f32[8,96,256]{2,1,0:T(8,128)S(1)} async-done(((f32[8,96,256]{2,1,0:T(8,128)}), f32[8,96,256]{2,1,0:T(8,128)S(1)}, u32[]{:S(2)}, u32[]{:S(2)}) %all-to-all-start.3) | async-done | bytes 786464 | tf_op jit(solution)/shard_map/all_to_all | solution.py:154
  301.5 0.9 copy-done.3
  302.3 2.1 shard_map.41
  304.4 3.7 %all-to-all-start.4 = ((f32[8,96,256]{2,1,0:T(8,128)}), f32[8,96,256]{2,1,0:T(8,128)S(1)}, u32[]{:S(2)}, u32[]{:S(2)}) async-start(f32[8,96,256]{2,1,0:T(8,128)} %shard_map.41), calls=%async_computation.4 | async-start | bytes 1572864 | tf_op jit(solution)/shard_map/all_to_all | solution.py:156
  308.2 0.3 fusion.2
  308.5 0.4 fusion.13.refs_4_
  308.9 0.4 fusion.14.refs_3_
  309.3 13.1 %all-to-all-done.4 = f32[8,96,256]{2,1,0:T(8,128)S(1)} async-done(((f32[8,96,256]{2,1,0:T(8,128)}), f32[8,96,256]{2,1,0:T(8,128)S(1)}, u32[]{:S(2)}, u32[]{:S(2)}) %all-to-all-start.4) | async-done | bytes 786464 | tf_op jit(solution)/shard_map/all_to_all | solution.py:156
  322.4 13.4 %shard_map.42 = f32[8192,256]{1,0:T(8,128)} custom-call(f32[2,256,8192]{2,1,0:T(8,128)} %all-gather.5.cloned.1.call-done.refs_0_.refs_1_, f32[2,256,8192]{2,1,0:T(8,128)} %all-gather.5.cloned.1.call-done.refs_0_.refs_1_, f32[768,256]{1,0:T(8,128)S(1)} %bitcast.41, f32[256,256]{1,0:T(8,128)S(1)} %fusion.14.refs_3_, f32[256,256]{1,0:T(8,128)S(1)} %fusion.13.refs_4_, ...), custom_call_target="tpu_custom_call" | custom-call | flops 6442450944 | bytes 33554432 | tf_op jit(solution)/shard_map/pallas_call | solution.py:133
  (24 shorter events, 0.2 us)
Async XLA Ops:
  6.5 2.3 copy-start
  6.5 41.3 %all-gather.9.cloned.1.call-start = ((), (), s32[]{:S(2)}) async-start(), calls=%async_computation.7 | async-start | bytes 4718592 | tf_op jit(solution)/shard_map/all_gather | solution.py:172
  8.8 190.6 %all-gather.7.cloned.1.call-start = ((), (), s32[]{:S(2)}) async-start(), calls=%async_computation.6 | async-start | bytes 9437184 | tf_op jit(solution)/shard_map/all_gather | solution.py:172
  9.0 36.6 %collective-permute-start = (f32[3,16,8192]{2,1,0:T(8,128)S(1)}, f32[3,16,8192]{2,1,0:T(8,128)S(1)}, u32[]{:S(2)}, u32[]{:S(2)}) collective-permute-start(f32[3,16,8192]{2,1,0:T(8,128)S(1)} %slice.41), channel_id=1, source_target_pairs={{0,8},{1,9},{2,10},{3,11},{4,12},{5,13},{6,14},{7,15},{8,0},{9,1},... | collective-permute-start | bytes 4718600 | tf_op jit(solution)/shard_map/ppermute | solution.py:168
  45.6 1.2 copy-start.1
  47.9 1.2 slice-start
  47.9 221.4 %all-gather.5.cloned.1.call-start = ((), (), s32[]{:S(2)}) async-start(), calls=%async_computation.5 | async-start | bytes 18874368 | tf_op jit(solution)/shard_map/all_gather | solution.py:172
  50.6 147.5 %all-to-all-start = ((f32[16,512,256]{2,1,0:T(8,128)}), f32[16,512,256]{2,1,0:T(8,128)}, u32[]{:S(2)}, u32[]{:S(2)}) async-start(f32[16,512,256]{2,1,0:T(8,128)} %bitcast.42), calls=%async_computation | async-start | bytes 16777216 | tf_op jit(solution)/shard_map/all_to_all | solution.py:208
  57.4 138.2 %copy-start.5 = (s32[16]{0:T(128)S(1)}, s32[16]{0:T(128)}, u32[]{:S(2)}) copy-start(s32[16]{0:T(128)} %constant.164.clone.1) | copy-start | bytes 196
  59.2 135.5 %collective-permute-start.1 = (f32[64,8192]{1,0:T(8,128)S(1)}, f32[64,8192]{1,0:T(8,128)S(1)}, u32[]{:S(2)}, u32[]{:S(2)}) collective-permute-start(f32[64,8192]{1,0:T(8,128)S(1)} %bitcast.50), channel_id=1, source_target_pairs={{0,8},{1,9},{2,10},{3,11},{4,12},{5,13},{6,14},{7,15},{8,0},{9,1},... | collective-permute-start | bytes 6291464 | tf_op jit(solution)/shard_map/ppermute | solution.py:168
  194.7 4.7 %collective-permute-start.2 = (f32[64,8192]{1,0:T(8,128)S(1)}, f32[64,8192]{1,0:T(8,128)}, u32[]{:S(2)}, u32[]{:S(2)}) collective-permute-start(f32[64,8192]{1,0:T(8,128)S(1)} %collective-permute-done.1.refs_2_), channel_id=1, source_target_pairs={{0,1},{1,0},{2,3},{3,2},{4,5},{5,4},{6,7},{7,6},{8,9},{9,8},{10,11... | collective-permute-start | bytes 6291464 | tf_op jit(solution)/shard_map/ppermute | solution.py:168
  199.4 21.6 %copy-start.6 = (s32[16]{0:T(128)S(1)}, s32[16]{0:T(128)}, u32[]{:S(2)}) copy-start(s32[16]{0:T(128)} %constant.162.clone.1) | copy-start | bytes 196
  213.5 21.8 %all-to-all-start.1 = ((f32[8,96,256]{2,1,0:T(8,128)}), f32[8,96,256]{2,1,0:T(8,128)S(1)}, u32[]{:S(2)}, u32[]{:S(2)}) async-start(f32[8,96,256]{2,1,0:T(8,128)} %bitcast.8), calls=%async_computation.1 | async-start | bytes 1572864 | tf_op jit(solution)/shard_map/all_to_all | solution.py:154
  235.3 0.9 copy-start.2
  238.3 18.0 %all-to-all-start.2 = ((f32[8,96,256]{2,1,0:T(8,128)}), f32[8,96,256]{2,1,0:T(8,128)S(1)}, u32[]{:S(2)}, u32[]{:S(2)}) async-start(f32[8,96,256]{2,1,0:T(8,128)} %shard_map.38), calls=%async_computation.2 | async-start | bytes 1572864 | tf_op jit(solution)/shard_map/all_to_all | solution.py:156
  269.3 17.7 %copy-start.4 = (f32[4,256,256]{2,1,0:T(8,128)S(1)}, f32[4,256,256]{2,1,0:T(8,128)}, u32[]{:S(2)}) copy-start(f32[4,256,256]{2,1,0:T(8,128)} %param.5) | copy-start | bytes 3145732
  283.4 18.0 %all-to-all-start.3 = ((f32[8,96,256]{2,1,0:T(8,128)}), f32[8,96,256]{2,1,0:T(8,128)S(1)}, u32[]{:S(2)}, u32[]{:S(2)}) async-start(f32[8,96,256]{2,1,0:T(8,128)} %bitcast.16), calls=%async_computation.3 | async-start | bytes 1572864 | tf_op jit(solution)/shard_map/all_to_all | solution.py:154
  301.4 0.9 copy-start.3
  304.4 18.0 %all-to-all-start.4 = ((f32[8,96,256]{2,1,0:T(8,128)}), f32[8,96,256]{2,1,0:T(8,128)S(1)}, u32[]{:S(2)}, u32[]{:S(2)}) async-start(f32[8,96,256]{2,1,0:T(8,128)} %shard_map.41), calls=%async_computation.4 | async-start | bytes 1572864 | tf_op jit(solution)/shard_map/all_to_all | solution.py:156
Sparse Core Ops, SparseCore 0:
  9.1 35.6 all-gather.8
  48.0 116.8 all-gather.6
  166.7 89.2 all-gather.4
